TPU v7x, 32 devices: a whole 2x2x4 slice. The times are simulated.
32 devices in a mesh: tm: 8 (over z, y), mp: 4 (over x, core).
Axes of the slice: x: 2, y: 2, z: 4, core: 2. Of those that a mesh axis runs over, the one named last changes fastest.
Arguments:
- frames_in: bfloat16 [4096, 1024], P('tm'), may hold values from -16 to 16
- queries: bfloat16 [4096, 1024], P('tm', 'mp'), may hold values from -6 to 6
- keys: bfloat16 [4096, 1024], P('tm', 'mp'), may hold values from -6 to 6
- values: bfloat16 [4096, 1024], P('tm', 'mp'), may hold values from -6 to 6
- segment_edges: int32 [2, 4096], P(None, 'tm'), may hold values from 0 to 4095, as said below
- out_proj: bfloat16 [1024, 1024], P('mp'), may hold values from -0.1875 to 0.1875
- expert_ids: int32 [4096, 2], P('tm'), may hold values from 0 to 15, all different within a row; in each aligned block of 512 rows (0 to 511, 512 to 1023, ...) at most 128 rows name the same one
- gates: float32 [4096, 2], P('tm'), may hold values from 0.25 to 1
- w_gate: bfloat16 [16, 1024, 4096], P('tm', None, 'mp'), may hold values from -0.1875 to 0.1875
- w_up: bfloat16 [16, 1024, 4096], P('tm', None, 'mp'), may hold values from -0.1875 to 0.1875
- w_down: bfloat16 [16, 4096, 1024], P('tm', 'mp'), may hold values from -0.09375 to 0.09375
Outputs:
- layer_out: bfloat16 [4096, 1024], P('tm', 'mp')
Inputs may be any that keep to these rules, and one draw needn't show every extreme that they name: `segment_edges`: row 0 holds the first frame of each frame's segment and row 1 its last. Segments are runs of 1 to 64 frames; every multiple of 64 starts a segment, and some segment has exactly 64 frames. `expert_ids`: each frame names 2 different experts. Among the 512 frames of one index of tm no expert is named more than 128 times; in some of these groups one expert is named exactly 128 times.
All inputs are finite; a program needn't handle non-finite values.
Results may differ from a plain program's by a relative error of at most 0.006.
Values may be sent and summed in bfloat16 or wider, within the bound.
No kernel may reach another device: no remote copies, remote signals or barrier semaphores. Data moves between devices by JAX's collectives and lax.ppermute only.
A program may use at most 128 MiB of HBM per device.

v0:
```python
import functools

import jax
import jax.numpy as jnp
from jax import lax
from jax.experimental import pallas as pl
from jax.experimental.pallas import tpu as pltpu
from jax.sharding import PartitionSpec as P

HEADS = 16
TOP = 2
LEFT = 256
EPS = 1e-06
LANES = 128
MIB = 1 << 20
F32 = jnp.float32
BF16 = jnp.bfloat16

VMEM = pl.BlockSpec(memory_space=pltpu.VMEM)
SMEM = pl.BlockSpec(memory_space=pltpu.SMEM)
ANY = pl.BlockSpec(memory_space=pl.ANY)
HBM = pl.BlockSpec(memory_space=pltpu.HBM)


def params(mib):
    return pltpu.CompilerParams(vmem_limit_bytes=mib * MIB)


def cost(flops, moved, transcendentals=0):
    return pl.CostEstimate(flops=flops, bytes_accessed=moved, transcendentals=transcendentals)


def from_behind(x, axis, by):
    size = lax.axis_size(axis)
    pairs = [(i, i + by) for i in range(size) if 0 <= i + by < size]
    return lax.ppermute(x, axis, pairs)


def core_swap(x):
    size = lax.axis_size("mp")
    return lax.ppermute(x, "mp", [(i, i ^ 1) for i in range(size)])


def from_chip(x, by):
    chips = lax.axis_size("mp") // 2
    pairs = [(c * 2 + k, ((c + by) % chips) * 2 + k) for c in range(chips) for k in range(2)]
    return lax.ppermute(x, "mp", pairs)


def gathered(x):
    chips = lax.axis_size("mp") // 2
    mine = [x] + [from_chip(x, by) for by in range(1, chips)]
    return mine + [core_swap(part) for part in mine]


def exchanged(blocks):
    size = lax.axis_size("tm")
    assert size & (size - 1) == 0, size
    moved = list(blocks)
    for s in range(size - 1, 0, -1):
        moved[s] = lax.ppermute(blocks[s], "tm", [(i, i ^ s) for i in range(size)])
    return moved


def route_kernel(capacity, local_experts, n_time, ids_ref, ranks_ref, targets_ref):
    frames = ids_ref.shape[0]
    lanes = ranks_ref.shape[0]
    ids = ids_ref[...]
    owner = ids // local_experts
    ids = (ids - owner * local_experts) * n_time + owner
    experts = lax.broadcasted_iota(jnp.int32, (frames, lanes), 1)
    hits = [ids[:, k : k + 1] == experts for k in range(TOP)]
    named = functools.reduce(jnp.logical_or, hits)
    ones = jnp.where(named, 1.0, 0.0).astype(BF16)
    row = lax.broadcasted_iota(jnp.int32, (frames, frames), 0)
    column = lax.broadcasted_iota(jnp.int32, (frames, frames), 1)
    before = jnp.where(column < row, 1.0, 0.0).astype(BF16)
    ranks = jnp.dot(before, ones, preferred_element_type=F32)
    ranks_ref[...] = jnp.where(named, ranks, -1.0).T
    places = []
    for k in range(TOP):
        slot = jnp.sum(jnp.where(hits[k], ranks, 0.0), 1, keepdims=True).astype(jnp.int32)
        places.append(ids[:, k : k + 1] * capacity + slot)
    targets_ref[...] = jnp.concatenate(places, 1)


def attend_kernel(scale, head_width, start, meta_ref, order_ref, *refs):
    if start > 0:
        edges_any, q_any, k_any, v_any, proj_any = refs[:5]
        send_ref, keep_x_ref, keep_ref, edges_ref, q_all, k_ref, v_ref, proj_ref, sems = refs[5:]
        moves = [
            (k_any, k_ref),
            (q_any, q_all),
            (v_any, v_ref),
            (edges_any, edges_ref),
            (proj_any, proj_ref),
        ]
    else:
        edges_ref, q_all, k_all, v_all, proj_ref, tails_any = refs[:6]
        send_ref, keep_x_ref, keep_ref, k_ref, v_ref, sems = refs[6:]
        first_rows = pl.ds(0, keep_ref.shape[0])
        moves = [
            (tails_any.at[0], k_ref.at[pl.ds(0, LEFT)]),
            (k_all.at[first_rows], k_ref.at[pl.ds(LEFT, keep_ref.shape[0])]),
            (tails_any.at[1], v_ref.at[pl.ds(0, LEFT)]),
            (v_all.at[first_rows], v_ref.at[pl.ds(LEFT, keep_ref.shape[0])]),
        ]
    rows, columns = keep_ref.shape
    heads = columns // head_width
    block = LANES
    window = LEFT + block
    copies = [pltpu.make_async_copy(a, b, sems.at[i]) for i, (a, b) in enumerate(moves)]
    for copy in copies:
        copy.start()
    for copy in copies[:4]:
        copy.wait()
    edges = edges_ref[:, start : start + rows].astype(F32)
    edges = jnp.concatenate([edges, jnp.zeros((6, rows), F32)], 0).T
    lane_head = lax.broadcasted_iota(jnp.int32, (block, columns), 1) // head_width
    context = []
    for r in range(0, rows, block):
        key = k_ref[r : r + window, :]
        value = v_ref[r : r + window, :]
        query = q_all[start + r : start + r + block, :]
        places = lax.broadcasted_iota(jnp.int32, (block, window), 1)
        places = (places + (meta_ref[0] + (start + r - LEFT))).astype(F32)
        lower = jnp.maximum(edges[r : r + block, 0:1] - LEFT, 0.0)
        upper = edges[r : r + block, 1:2]
        visible = (places >= lower) & (places <= upper)
        own = [jnp.where(lane_head == h, query, jnp.zeros_like(query)) for h in range(heads)]
        own = jnp.concatenate(own, 0)
        scores = lax.dot_general(own, key, (((1,), (1,)), ((), ())), preferred_element_type=F32)
        scores = (scores * scale).reshape(heads, block, window)
        scores = jnp.where(visible[None], scores, -1e30)
        highest = jnp.max(scores, 2, keepdims=True)
        expos = jnp.exp(scores - highest)
        weights = (expos * (1.0 / jnp.sum(expos, 2, keepdims=True))).astype(BF16)
        weights = weights.reshape(heads * block, window)
        product = jnp.dot(weights, value, preferred_element_type=F32)
        mixed = product[0:block]
        for h in range(1, heads):
            mixed = jnp.where(lane_head == h, product[h * block : (h + 1) * block], mixed)
        context.append(mixed.astype(BF16))
    context = jnp.concatenate(context, 0)
    for copy in copies[4:]:
        copy.wait()
    count = proj_ref.shape[1] // columns // 2
    for i in range(2 * count):
        at = pl.multiple_of(order_ref[i] * columns, columns)
        part = jnp.dot(context, proj_ref[:, pl.ds(at, columns)], preferred_element_type=F32)
        j = (i - 1) % count * columns
        if i >= count:
            send_ref[:, j : j + columns] = part.astype(BF16)
        elif i > 0:
            keep_x_ref[:, j : j + columns] = part
        else:
            keep_ref[...] = part


def picked_rows(e, capacity, ranks_ref, state):
    slot = lax.broadcasted_iota(jnp.int32, (capacity, state.shape[0]), 0).astype(F32)
    pick = jnp.where(slot == ranks_ref[pl.ds(e, 1), :], 1.0, 0.0).astype(BF16)
    return jnp.dot(pick, state, preferred_element_type=F32).astype(BF16)


def scatter_rows(local, at_ref, ranks_ref, state, out_refs):
    n_time = len(out_refs)
    for s, out_ref in enumerate(out_refs):
        owner = at_ref[0] ^ s
        out_ref[...] = picked_rows(local * n_time + owner, out_ref.shape[0], ranks_ref, state)


def state_kernel(parts, column, at_ref, *refs):
    frames_ref, ranks_ref, state_ref = refs[2 * parts : 2 * parts + 3]
    width = state_ref.shape[1]
    halves = []
    for keep_ref, swapped_ref, *got in (refs[:parts], refs[parts : 2 * parts]):
        half = keep_ref[...] + swapped_ref[:, column : column + width].astype(F32)
        for ref in got:
            half = half + ref[...].astype(F32)
        halves.append(half)
    attended = jnp.concatenate(halves, 0)
    state = (frames_ref[...].astype(F32) + attended).astype(BF16)
    state_ref[...] = state
    scatter_rows(0, at_ref, ranks_ref, state, refs[2 * parts + 3 :])


def dispatch_kernel(pieces, n_time, *refs):
    state = jnp.concatenate([ref[...] for ref in refs[:pieces]], 1)
    ranks_ref, out_ref = refs[pieces:]
    capacity = out_ref.shape[0] // n_time
    for owner in range(n_time):
        rows = picked_rows(n_time + owner, capacity, ranks_ref, state)
        out_ref[owner * capacity : (owner + 1) * capacity, :] = rows


def join_kernel(*refs):
    *pieces, after_any, out_ref = refs
    count = pieces[0].shape[0]
    for s, ref in enumerate(pieces):
        out_ref[s * count : (s + 1) * count, :] = ref[...]


def take_kernel(rows_ref, *refs):
    refs[-1][...] = rows_ref[...]


def expert_kernel(local, starts, width, awaited, order_ref, *refs):
    arrays = len(starts)
    rows_in = refs[:arrays]
    gate_any, up_any, down_any = refs[arrays : arrays + 3]
    *outs, gate_ref, up_ref, down_ref, normed_ref, active_ref, sems = refs[arrays + 3 + awaited :]
    *send_x_refs, send_ref, keep_x_ref, keep_ref = outs
    rows, model = normed_ref.shape
    hidden = active_ref.shape[1]
    moves = [
        (gate_any.at[local], gate_ref),
        (up_any.at[local], up_ref),
        (down_any.at[local], down_ref),
    ]
    copies = [pltpu.make_async_copy(a, b, sems.at[i]) for i, (a, b) in enumerate(moves)]
    for copy in copies:
        copy.start()

    blocks = []
    for ref, start in zip(rows_in, starts):
        blocks += [(ref, start, c) for c in range(0, ref.shape[1], width)]
    step = min(rows, 256)

    def norm(i, carry):
        at_row = pl.multiple_of(i * step, step)
        parts = [
            ref[pl.ds(pl.multiple_of(start + i * step, step), step), c : c + width].astype(F32)
            for ref, start, c in blocks
        ]
        squares = sum(jnp.sum(part * part, 1, keepdims=True) for part in parts)
        factor = lax.rsqrt(squares * (1.0 / model) + EPS)
        for j, part in enumerate(parts):
            at = pl.multiple_of(order_ref[j] * width, width)
            normed_ref[pl.ds(at_row, step), pl.ds(at, width)] = (part * factor).astype(BF16)
        return carry

    lax.fori_loop(0, rows // step, norm, 0)
    copies[0].wait()
    copies[1].wait()
    tile = min(rows, 1024)
    chunk = min(hidden, 256)
    for r in range(0, rows, tile):
        normed = normed_ref[r : r + tile, :]
        for c in range(0, hidden, chunk):
            gate = jnp.dot(normed, gate_ref[:, c : c + chunk], preferred_element_type=F32)
            up = jnp.dot(normed, up_ref[:, c : c + chunk], preferred_element_type=F32)
            half = 0.5 * gate
            active = (half + half * jnp.tanh(half)) * up
            active_ref[r : r + tile, c : c + chunk] = active.astype(BF16)
    copies[2].wait()
    count = len(blocks) // 2
    def project(i, out_refs, column):
        at = pl.multiple_of(order_ref[i] * width, width)
        weight = down_ref[:, pl.ds(at, width)]
        result = jnp.dot(active_ref[...], weight, preferred_element_type=F32)
        each = rows // len(out_refs)
        for j, out_ref in enumerate(out_refs):
            part = result[j * each : (j + 1) * each]
            out_ref[:, column : column + width] = part.astype(out_ref.dtype)

    for by in range(1, count):
        project(count + by, send_x_refs, (by - 1) * width)
    project(count, [send_ref], 0)
    for by in range(1, count):
        project(by, [keep_x_ref], (by - 1) * width)
    project(0, [keep_ref], 0)


def add_kernel(width, keep_ref, got_ref, after_any, *out_refs):
    for i, out_ref in enumerate(out_refs):
        at = slice(i * width, (i + 1) * width)
        out_ref[...] = (keep_ref[:, at] + got_ref[:, at].astype(F32)).astype(BF16)


def spread_kernel(n_time, awaited, turned, at_ref, keep_ref, *refs):
    got, outs = refs[: -n_time - awaited], refs[-n_time:]
    capacity = outs[0].shape[0]
    for s, out_ref in enumerate(outs):
        place = at_ref[0] ^ s if turned else s
        at = pl.ds(pl.multiple_of(place * capacity, capacity), capacity)
        total = keep_ref[at, :]
        for ref in got:
            total = total + ref[at, :].astype(F32)
        out_ref[...] = total.astype(BF16)


def combine_kernel(local, at_ref, targets_ref, gates_ref, base_ref, *refs):
    *got, out_ref, back_ref = refs
    capacity = got[0].shape[0]
    for s, ref in enumerate(reversed(got)):
        place = at_ref[0] ^ s
        back_ref[pl.ds(pl.multiple_of(place * capacity, capacity), capacity), :] = ref[...]
    back = back_ref[...]
    rows = back.shape[0]
    frames = targets_ref.shape[0]
    places = lax.broadcasted_iota(jnp.int32, (frames, rows), 1) + local * rows
    total = base_ref[...].astype(F32)
    for k in range(TOP):
        pick = jnp.where(places == targets_ref[:, k : k + 1], 1.0, 0.0).astype(BF16)
        total = total + gates_ref[:, k : k + 1] * jnp.dot(pick, back, preferred_element_type=F32)
    out_ref[...] = total.astype(out_ref.dtype)


def per_device(
    frames_in,
    queries,
    keys,
    values,
    segment_edges,
    out_proj,
    expert_ids,
    gates,
    w_gate,
    w_up,
    w_down,
):
    frames, model = frames_in.shape
    width = queries.shape[1]
    n_model = lax.axis_size("mp")
    n_time = lax.axis_size("tm")
    chips = n_model // 2
    head_width = model // HEADS
    scale = head_width ** (-0.5)
    local_experts = w_gate.shape[0]
    hidden = w_gate.shape[2]
    experts_all = local_experts * n_time
    capacity = 4 * frames // experts_all
    rows = n_time * capacity
    lanes = -(-experts_all // LANES) * LANES
    at_time = lax.axis_index("tm")
    at_model = lax.axis_index("mp")
    chip, core = at_model // 2, at_model % 2
    mine = [((chip - by) % chips) * 2 + core for by in range(chips)]
    others = [((chip - by) % chips) * 2 + 1 - core for by in range(chips)]
    order = jnp.stack(mine + others).astype(jnp.int32)
    offset = (at_time * frames).astype(jnp.int32).reshape(1)
    place = at_time.astype(jnp.int32).reshape(1)
    away = (chips - 1) * width

    tails = from_behind(jnp.stack([keys[frames - LEFT :], values[frames - LEFT :]], 0), "tm", 1)
    own_frames = lax.dynamic_slice_in_dim(frames_in, at_model * width, width, 1)

    ranks, targets = pl.pallas_call(
        functools.partial(route_kernel, capacity, local_experts, n_time),
        out_shape=(
            jax.ShapeDtypeStruct((lanes, frames), F32),
            jax.ShapeDtypeStruct((frames, TOP), jnp.int32),
        ),
        in_specs=[VMEM],
        out_specs=(VMEM, VMEM),
        compiler_params=params(16),
        cost_estimate=cost(2 * frames * frames * lanes, frames * 1024),
        name="route",
    )(expert_ids)

    def in_hbm(*arrays):
        return [pltpu.with_memory_space_constraint(x, pltpu.HBM) for x in arrays]

    def attended_outs(count):
        return (
            jax.ShapeDtypeStruct((count, chips * width), BF16),
            jax.ShapeDtypeStruct((count, away), F32),
            jax.ShapeDtypeStruct((count, width), F32),
        )

    def attend_cost(count):
        return cost(count * 384 * width * 16, count * width * 8, count * 384 * 4)

    inputs = (segment_edges, queries, keys, values, out_proj)
    *late, edges_vmem, q_vmem, k_vmem, v_vmem, proj_vmem = pl.pallas_call(
        functools.partial(attend_kernel, scale, head_width, LEFT),
        out_shape=attended_outs(frames - LEFT)
        + tuple(jax.ShapeDtypeStruct(x.shape, x.dtype) for x in inputs),
        in_specs=[SMEM, SMEM] + [HBM] * 5,
        out_specs=(VMEM,) * 8,
        scratch_shapes=[pltpu.SemaphoreType.DMA((5,))],
        compiler_params=params(16),
        cost_estimate=attend_cost(frames - LEFT),
        name="attend_late",
    )(offset, order, *in_hbm(*inputs))
    early = pl.pallas_call(
        functools.partial(attend_kernel, scale, head_width, 0),
        out_shape=attended_outs(LEFT),
        in_specs=[SMEM, SMEM] + [VMEM] * 5 + [ANY],
        out_specs=(VMEM,) * 3,
        scratch_shapes=[
            pltpu.VMEM((2 * LEFT, width), BF16),
            pltpu.VMEM((2 * LEFT, width), BF16),
            pltpu.SemaphoreType.DMA((4,)),
        ],
        compiler_params=params(16),
        cost_estimate=attend_cost(LEFT),
        name="attend_early",
    )(offset, order, edges_vmem, q_vmem, k_vmem, v_vmem, proj_vmem, tails)

    def add(name, keep, got, after):
        return pl.pallas_call(
            functools.partial(add_kernel, width),
            in_specs=[VMEM, VMEM, ANY],
            out_specs=(VMEM,) * (chips - 1),
            out_shape=(jax.ShapeDtypeStruct((keep.shape[0], width), BF16),) * (chips - 1),
            compiler_params=params(16),
            cost_estimate=cost(keep.size, keep.size * 8),
            name=f"add_{name}",
        )(keep, got, after)

    def from_chips(parts):
        return [from_chip(part, chips - by) for by, part in enumerate(parts, 1)]

    def attended(name, send, keep_x, keep):
        swapped = core_swap(send)
        return [keep, swapped, *from_chips(add(name, keep_x, swapped, swapped))]

    late = attended("late", *late)
    early = attended("early", *early)

    def blocks_of(count):
        return (jax.ShapeDtypeStruct((capacity, width), BF16),) * count

    state, *outgoing_0 = pl.pallas_call(
        functools.partial(state_kernel, len(early), away),
        out_shape=(jax.ShapeDtypeStruct((frames, width), BF16),) + blocks_of(n_time),
        in_specs=[SMEM] + [VMEM] * (2 * len(early) + 2),
        out_specs=(VMEM,) * (1 + n_time),
        compiler_params=params(16),
        cost_estimate=cost(2 * frames * width * rows, 4 * MIB),
        name="state",
    )(place, *early, *late, own_frames, ranks)
    wide = [state] + [from_chip(state, by) for by in range(1, chips)]
    outgoing_1 = pl.pallas_call(
        functools.partial(dispatch_kernel, chips, n_time),
        out_shape=jax.ShapeDtypeStruct((rows, chips * width), BF16),
        in_specs=[VMEM] * (chips + 1),
        out_specs=VMEM,
        compiler_params=params(16),
        cost_estimate=cost(4 * frames * width * rows, 3 * MIB),
        name="dispatch",
    )(*wide, ranks)

    def over_time(x):
        columns = x.shape[1]
        x = x.reshape(n_time, capacity, columns)
        x = lax.all_to_all(x, "tm", split_axis=0, concat_axis=0, tiled=True)
        return x.reshape(rows, columns)

    def take(x, after):
        return pl.pallas_call(
            take_kernel,
            in_specs=[VMEM] + [ANY] * len(after),
            out_specs=VMEM,
            out_shape=jax.ShapeDtypeStruct(x.shape, x.dtype),
            compiler_params=params(16),
            cost_estimate=cost(x.size, x.size * 4),
            name="take",
        )(x, *after)

    def experts(local, parts, after):
        outs = [jax.ShapeDtypeStruct((rows, columns), BF16) for columns in (away, width)]
        outs += [jax.ShapeDtypeStruct((rows, columns), F32) for columns in (away, width)]
        return pl.pallas_call(
            functools.partial(expert_kernel, local, (0,) * len(parts), width, len(after)),
            in_specs=[SMEM] + [VMEM] * len(parts) + [HBM] * 3 + [ANY] * len(after),
            out_specs=(VMEM,) * 4,
            scratch_shapes=[
                pltpu.VMEM((model, hidden), BF16),
                pltpu.VMEM((model, hidden), BF16),
                pltpu.VMEM((hidden, model), BF16),
                pltpu.VMEM((rows, model), BF16),
                pltpu.VMEM((rows, hidden), BF16),
                pltpu.SemaphoreType.DMA((3,)),
            ],
            out_shape=tuple(outs),
            compiler_params=params(20),
            cost_estimate=cost(6 * rows * model * hidden, 12 * MIB, rows * hidden),
            name=f"experts_{local}",
        )(order, *parts, *in_hbm(w_gate, w_up, w_down), *after)

    def spread(local, turned, parts, after):
        return pl.pallas_call(
            functools.partial(spread_kernel, n_time, len(after), turned),
            in_specs=[SMEM] + [VMEM] * len(parts) + [ANY] * len(after),
            out_specs=(VMEM,) * n_time,
            out_shape=blocks_of(n_time),
            compiler_params=params(16),
            cost_estimate=cost(rows * width * 4, rows * width * 10),
            name=f"spread_{local}",
        )(place, *parts, *after)

    def combine(local, back, base):
        last = local == local_experts - 1
        return pl.pallas_call(
            functools.partial(combine_kernel, local),
            out_shape=jax.ShapeDtypeStruct((frames, width), BF16 if last else F32),
            in_specs=[SMEM] + [VMEM] * (3 + len(back)),
            out_specs=VMEM,
            scratch_shapes=[pltpu.VMEM((rows, width), BF16)],
            compiler_params=params(16),
            cost_estimate=cost(4 * frames * width * rows, 3 * MIB),
            name=f"combine_{local}",
        )(place, targets, gates, base, *reversed(back))

    outgoing_0[1] = take(outgoing_0[1], wide[1:])
    arrived_0 = pl.pallas_call(
        join_kernel,
        in_specs=[VMEM] * n_time + [ANY],
        out_specs=VMEM,
        out_shape=jax.ShapeDtypeStruct((rows, width), BF16),
        compiler_params=params(16),
        cost_estimate=cost(rows * width, rows * width * 4),
        name="join",
    )(*exchanged(outgoing_0), outgoing_1)
    arrived_1 = over_time(outgoing_1)
    send_x_0, send_0, keep_x_0, keep_0 = experts(0, gathered(arrived_0), [outgoing_1])
    away_0 = add("0", keep_x_0, core_swap(send_x_0), send_0)
    got_0 = from_chips(away_0)
    swapped_0 = core_swap(send_0)
    arrived_1 = take(arrived_1, [away_0[0]])
    parts = [arrived_1, core_swap(arrived_1)]
    send_x_1, send_1, keep_x_1, keep_1 = experts(1, parts, [away_0[0]])
    away_1 = add("1", keep_x_1, core_swap(send_x_1), got_0[0])
    got_1 = from_chips(away_1)
    total_0 = spread(0, False, [keep_0, swapped_0, *got_0], [away_1[0]])
    back_0 = exchanged(total_0)
    total_1 = spread(1, True, [keep_1, core_swap(send_1), *got_1], back_0[n_time // 2 + 1 :])
    back_1 = exchanged(total_1)
    return combine(1, back_1, combine(0, back_0, state))


def solution(mesh):
    return jax.shard_map(
        per_device,
        mesh=mesh,
        in_specs=(
            P("tm", None),
            P("tm", "mp"),
            P("tm", "mp"),
            P("tm", "mp"),
            P(None, "tm"),
            P("mp", None),
            P("tm", None),
            P("tm", None),
            P("tm", None, "mp"),
            P("tm", None, "mp"),
            P("tm", "mp", None),
        ),
        out_specs=P("tm", "mp"),
        check_vma=False,
    )
```

profile of v0, /device:TPU:0, one launch (start us, length us, event | category | flops | bytes accessed | tf_op | source)
XLA Modules:
  0.0 120.0 jit_solution(15109448994639036122)
XLA Ops:
  1.1 4.9 %collective-permute-start = (bf16[2,256,256]{2,1,0:T(8,128)(2,1)S(1)}, bf16[2,256,256]{2,1,0:T(8,128)(2,1)S(1)}, u32[]{:S(2)}, u32[]{:S(2)}) collective-permute-start(bf16[2,256,256]{2,1,0:T(8,128)(2,1)S(1)} %pad_maximum_fusion), channel_id=1, source_target_pairs={{0,4},{4,8},{8,12},{12,16},{16,20},{20,24},{24,28},{1,5},{5,9},{9,... | collective-permute-start | bytes 786440 | tf_op jit(solution)/shard_map/ppermute | solution.py:36
  6.2 3.5 %attend_late.1 = (bf16[256,512]{1,0:T(8,128)(2,1)S(1)}, f32[256,256]{1,0:T(8,128)S(1)}, f32[256,256]{1,0:T(8,128)S(1)}, s32[2,512]{1,0:T(2,128)S(1)}, bf16[512,2...) custom-call(s32[1]{0:T(128)} %bitcast.1.meta_ref, ...), custom_call_target="tpu_custom_call" | custom-call | flops 402653184 | bytes 524288 | tf_op jit(solution)/shard_map/attend_late/pallas_call | solution.py:376
  9.8 1.8 %collective-permute-done.refs_5_ = bf16[2,256,256]{2,1,0:T(8,128)(2,1)S(1)} collective-permute-done((bf16[2,256,256]{2,1,0:T(8,128)(2,1)S(1)}, bf16[2,256,256]{2,1,0:T(8,128)(2,1)S(1)}, u32[]{:S(2)}, u32[]{:S(2)}) %collective-permute-start) | collective-permute-done | bytes 262176 | tf_op jit(solution)/shard_map/ppermute | solution.py:36
  11.6 3.0 %attend_early.1 = (bf16[256,512]{1,0:T(8,128)(2,1)S(1)}, f32[256,256]{1,0:T(8,128)S(1)}, f32[256,256]{1,0:T(8,128)S(1)}) custom-call(s32[1]{0:T(128)} %bitcast.1.meta_ref, s32[4]{0:T(128)S(1)} %pad_add_fusion.order_ref, s32[2,512]{1,0:T(2,128)S(1)} %get-tuple-element.52.refs_0_, bf16[512,256]{1,0:T(8,128)(2,1)S(1)} %get-tuple-element.53.refs_1_, ...), custom_call_target="tpu_custom_call" | custom-call | flops 402653184 | bytes 524288 | tf_op jit(solution)/shard_map/attend_early/pallas_call | solution.py:387
  14.7 1.6 %collective-permute-start.4 = (bf16[256,256]{1,0:T(8,128)(2,1)S(1)}, bf16[256,256]{1,0:T(8,128)(2,1)S(1)}, u32[]{:S(2)}, u32[]{:S(2)}) collective-permute-start(bf16[256,256]{1,0:T(8,128)(2,1)S(1)} %add_late.1), channel_id=1, source_target_pairs={{0,2},{1,3},{2,0},{3,1},{4,6},{5,7},{6,4},{7,5},{8,10},{9,11},{10,... | collective-permute-start | bytes 393224 | tf_op jit(solution)/shard_map/ppermute | solution.py:47
  16.3 1.5 %collective-permute-start.2 = (bf16[256,256]{1,0:T(8,128)(2,1)S(1)}, bf16[256,256]{1,0:T(8,128)(2,1)S(1)}, u32[]{:S(2)}, u32[]{:S(2)}) collective-permute-start(bf16[256,256]{1,0:T(8,128)(2,1)S(1)} %add_early.1), channel_id=1, source_target_pairs={{0,2},{1,3},{2,0},{3,1},{4,6},{5,7},{6,4},{7,5},{8,10},{9,11},{10,... | collective-permute-start | bytes 393224 | tf_op jit(solution)/shard_map/ppermute | solution.py:47
  18.8 2.2 %collective-permute-done.4.refs_5_ = bf16[256,256]{1,0:T(8,128)(2,1)S(1)} collective-permute-done((bf16[256,256]{1,0:T(8,128)(2,1)S(1)}, bf16[256,256]{1,0:T(8,128)(2,1)S(1)}, u32[]{:S(2)}, u32[]{:S(2)}) %collective-permute-start.4) | collective-permute-done | bytes 131104 | tf_op jit(solution)/shard_map/ppermute | solution.py:47
  21.0 2.4 %collective-permute-done.2.refs_2_ = bf16[256,256]{1,0:T(8,128)(2,1)S(1)} collective-permute-done((bf16[256,256]{1,0:T(8,128)(2,1)S(1)}, bf16[256,256]{1,0:T(8,128)(2,1)S(1)}, u32[]{:S(2)}, u32[]{:S(2)}) %collective-permute-start.2) | collective-permute-done | bytes 131104 | tf_op jit(solution)/shard_map/ppermute | solution.py:47
  24.0 1.5 %collective-permute-start.5 = (bf16[512,256]{1,0:T(8,128)(2,1)S(1)}, bf16[512,256]{1,0:T(8,128)(2,1)S(1)}, u32[]{:S(2)}, u32[]{:S(2)}) collective-permute-start(bf16[512,256]{1,0:T(8,128)(2,1)S(1)} %get-tuple-element.64.refs_0_.base_ref), channel_id=1, source_target_pairs={{0,2},{1,3},{2,0},{3,1},{4,6},{5,7},{6,4},{7,5},{8,10},{9,11},{10,... | collective-permute-start | bytes 786440 | tf_op jit(solution)/shard_map/ppermute | solution.py:47
  25.5 4.5 %collective-permute-start.10 = (bf16[128,256]{1,0:T(8,128)(2,1)S(1)}, bf16[128,256]{1,0:T(8,128)(2,1)S(1)}, u32[]{:S(2)}, u32[]{:S(2)}) collective-permute-start(bf16[128,256]{1,0:T(8,128)(2,1)S(1)} %get-tuple-element.70), channel_id=1, source_target_pairs={{0,20},{4,16},{8,28},{12,24},{16,4},{20,0},{24,12},{28,8},{1,21},{... | collective-permute-start | bytes 196616 | tf_op jit(solution)/shard_map/ppermute | solution.py:61
  31.4 3.3 %collective-permute-start.12 = (bf16[128,256]{1,0:T(8,128)(2,1)S(1)}, bf16[128,256]{1,0:T(8,128)(2,1)S(1)}, u32[]{:S(2)}, u32[]{:S(2)}) collective-permute-start(bf16[128,256]{1,0:T(8,128)(2,1)S(1)} %get-tuple-element.72), channel_id=1, source_target_pairs={{0,28},{4,24},{8,20},{12,16},{16,12},{20,8},{24,4},{28,0},{1,29},{... | collective-permute-start | bytes 196616 | tf_op jit(solution)/shard_map/ppermute | solution.py:61
  34.7 2.1 %collective-permute-start.8 = (bf16[128,256]{1,0:T(8,128)(2,1)S(1)}, bf16[128,256]{1,0:T(8,128)(2,1)S(1)}, u32[]{:S(2)}, u32[]{:S(2)}) collective-permute-start(bf16[128,256]{1,0:T(8,128)(2,1)S(1)} %get-tuple-element.68), channel_id=1, source_target_pairs={{0,12},{4,8},{8,4},{12,0},{16,28},{20,24},{24,20},{28,16},{1,13},{... | collective-permute-start | bytes 196616 | tf_op jit(solution)/shard_map/ppermute | solution.py:61
  38.1 1.4 %collective-permute-start.6 = (bf16[128,256]{1,0:T(8,128)(2,1)S(1)}, bf16[128,256]{1,0:T(8,128)(2,1)S(1)}, u32[]{:S(2)}, u32[]{:S(2)}) collective-permute-start(bf16[128,256]{1,0:T(8,128)(2,1)S(1)} %take.2), channel_id=1, source_target_pairs={{0,4},{4,0},{8,12},{12,8},{16,20},{20,16},{24,28},{28,24},{1,5},{5... | collective-permute-start | bytes 196616 | tf_op jit(solution)/shard_map/ppermute | solution.py:61
  39.5 1.7 %dispatch.1.refs_8_.refs_7_ = bf16[1024,512]{1,0:T(8,128)(2,1)} custom-call(bf16[512,256]{1,0:T(8,128)(2,1)S(1)} %get-tuple-element.64.refs_0_.base_ref, bf16[512,256]{1,0:T(8,128)(2,1)S(1)} %collective-permute-done.5.refs_0_.refs_1_, f32[128,512]{1,0:T(8,128)S(1)} %get-tuple-element.63.refs_7_.refs_2_), custom_call_target="tpu_custom_call" | custom-call | flops 536870912 | bytes 3145728 | tf_op jit(solution)/shard_map/dispatch/pallas_call | solution.py:436
  41.3 1.5 %collective-permute-done.9.refs_4_ = bf16[128,256]{1,0:T(8,128)(2,1)S(1)} collective-permute-done((bf16[128,256]{1,0:T(8,128)(2,1)S(1)}, bf16[128,256]{1,0:T(8,128)(2,1)S(1)}, u32[]{:S(2)}, u32[]{:S(2)}) %collective-permute-start.9) | collective-permute-done | bytes 65568 | tf_op jit(solution)/shard_map/ppermute | solution.py:61
  44.0 3.8 %all-to-all-start = ((bf16[8,128,512]{2,1,0:T(8,128)(2,1)}), bf16[8,128,512]{2,1,0:T(8,128)(2,1)S(1)}, u32[]{:S(2)}, u32[]{:S(2)}) async-start(bf16[8,128,512]{2,1,0:T(8,128)(2,1)} %bitcast.8), calls=%async_computation | async-start | bytes 2097152 | tf_op jit(solution)/shard_map/all_to_all | solution.py:449
  47.8 6.4 %collective-permute-done.13.refs_1_ = bf16[1024,256]{1,0:T(8,128)(2,1)S(1)} collective-permute-done((bf16[1024,256]{1,0:T(8,128)(2,1)S(1)}, bf16[1024,256]{1,0:T(8,128)(2,1)S(1)}, u32[]{:S(2)}, u32[]{:S(2)}) %collective-permute-start.13) | collective-permute-done | bytes 524320 | tf_op jit(solution)/shard_map/ppermute | solution.py:47
  57.1 9.7 %experts_0.1 = (bf16[1024,256]{1,0:T(8,128)(2,1)S(1)}, bf16[1024,256]{1,0:T(8,128)(2,1)S(1)}, f32[1024,256]{1,0:T(8,128)S(1)}, f32[1024,256]{1,0:T(8,128)S(1)}) custom-call(s32[4]{0:T(128)S(1)} %pad_add_fusion.order_ref, bf16[1024,256]{1,0:T(8,128)(2,1)S(1)} %join.1.refs_0_, bf16[1024,256]{1,0:T(8,128)(2,1)S(1)} %copy-done.4, ...), custom_call_target="tpu_custom_call" | custom-call | flops 6442450944 | bytes 12582912 | tf_op jit(solution)/shard_map/experts_0/pallas_call | solution.py:466
  67.9 1.8 %collective-permute-done.17.got_ref = bf16[1024,256]{1,0:T(8,128)(2,1)S(1)} collective-permute-done((bf16[1024,256]{1,0:T(8,128)(2,1)S(1)}, bf16[1024,256]{1,0:T(8,128)(2,1)S(1)}, u32[]{:S(2)}, u32[]{:S(2)}) %collective-permute-start.17) | collective-permute-done | bytes 524320 | tf_op jit(solution)/shard_map/ppermute | solution.py:41
  69.8 3.2 %all-to-all-done = bf16[8,128,512]{2,1,0:T(8,128)(2,1)S(1)} async-done(((bf16[8,128,512]{2,1,0:T(8,128)(2,1)}), bf16[8,128,512]{2,1,0:T(8,128)(2,1)S(1)}, u32[]{:S(2)}, u32[]{:S(2)}) %all-to-all-start) | async-done | bytes 1048608 | tf_op jit(solution)/shard_map/all_to_all | solution.py:449
  73.2 1.8 %collective-permute-start.18 = (bf16[1024,256]{1,0:T(8,128)(2,1)S(1)}, bf16[1024,256]{1,0:T(8,128)(2,1)S(1)}, u32[]{:S(2)}, u32[]{:S(2)}) collective-permute-start(bf16[1024,256]{1,0:T(8,128)(2,1)S(1)} %add_0.1.refs_0_.refs_5_), channel_id=1, source_target_pairs={{0,2},{1,3},{2,0},{3,1},{4,6},{5,7},{6,4},{7,5},{8,10},{9,11},{10,... | collective-permute-start | bytes 1572872 | tf_op jit(solution)/shard_map/ppermute | solution.py:47
  75.8 9.7 %experts_1.1 = (bf16[1024,256]{1,0:T(8,128)(2,1)S(1)}, bf16[1024,256]{1,0:T(8,128)(2,1)S(1)}, f32[1024,256]{1,0:T(8,128)S(1)}, f32[1024,256]{1,0:T(8,128)S(1)}) custom-call(s32[4]{0:T(128)S(1)} %pad_add_fusion.order_ref, bf16[1024,512]{1,0:T(8,128)(2,1)S(1)} %take.3.refs_0_, bf16[1024,512]{1,0:T(8,128)(2,1)S(1)} %collective-permute-done.19.refs_1_, ...), custom_call_target="tpu_custom_call" | custom-call | flops 6442450944 | bytes 12582912 | tf_op jit(solution)/shard_map/experts_1/pallas_call | solution.py:466
  87.6 1.8 %collective-permute-start.29 = (bf16[1024,256]{1,0:T(8,128)(2,1)S(1)}, bf16[1024,256]{1,0:T(8,128)(2,1)S(1)}, u32[]{:S(2)}, u32[]{:S(2)}) collective-permute-start(bf16[1024,256]{1,0:T(8,128)(2,1)S(1)} %add_1.1.refs_2_), channel_id=1, source_target_pairs={{0,2},{1,3},{2,0},{3,1},{4,6},{5,7},{6,4},{7,5},{8,10},{9,11},{10,... | collective-permute-start | bytes 1572872 | tf_op jit(solution)/shard_map/ppermute | solution.py:47
  89.6 2.2 %collective-permute-start.21 = (bf16[128,256]{1,0:T(8,128)(2,1)S(1)}, bf16[128,256]{1,0:T(8,128)(2,1)S(1)}, u32[]{:S(2)}, u32[]{:S(2)}) collective-permute-start(bf16[128,256]{1,0:T(8,128)(2,1)S(1)} %get-tuple-element.79), channel_id=1, source_target_pairs={{0,28},{4,24},{8,20},{12,16},{16,12},{20,8},{24,4},{28,0},{1,29},{... | collective-permute-start | bytes 196616 | tf_op jit(solution)/shard_map/ppermute | solution.py:61
  91.8 2.4 %collective-permute-start.22 = (bf16[128,256]{1,0:T(8,128)(2,1)S(1)}, bf16[128,256]{1,0:T(8,128)(2,1)S(1)}, u32[]{:S(2)}, u32[]{:S(2)}) collective-permute-start(bf16[128,256]{1,0:T(8,128)(2,1)S(1)} %get-tuple-element.80), channel_id=1, source_target_pairs={{0,24},{4,28},{8,16},{12,20},{16,8},{20,12},{24,0},{28,4},{1,25},{... | collective-permute-start | bytes 196616 | tf_op jit(solution)/shard_map/ppermute | solution.py:61
  94.2 3.2 %collective-permute-start.24 = (bf16[128,256]{1,0:T(8,128)(2,1)S(1)}, bf16[128,256]{1,0:T(8,128)(2,1)S(1)}, u32[]{:S(2)}, u32[]{:S(2)}) collective-permute-start(bf16[128,256]{1,0:T(8,128)(2,1)S(1)} %get-tuple-element.82), channel_id=1, source_target_pairs={{0,16},{4,20},{8,24},{12,28},{16,0},{20,4},{24,8},{28,12},{1,17},{... | collective-permute-start | bytes 196616 | tf_op jit(solution)/shard_map/ppermute | solution.py:61
  101.4 2.2 %collective-permute-start.27 = (bf16[128,256]{1,0:T(8,128)(2,1)S(1)}, bf16[128,256]{1,0:T(8,128)(2,1)S(1)}, u32[]{:S(2)}, u32[]{:S(2)}) collective-permute-start(bf16[128,256]{1,0:T(8,128)(2,1)S(1)} %get-tuple-element.85), channel_id=1, source_target_pairs={{0,4},{4,0},{8,12},{12,8},{16,20},{20,16},{24,28},{28,24},{1,5},{5... | collective-permute-start | bytes 196616 | tf_op jit(solution)/shard_map/ppermute | solution.py:61
  105.2 2.0 %collective-permute-start.31 = (bf16[128,256]{1,0:T(8,128)(2,1)S(1)}, bf16[128,256]{1,0:T(8,128)(2,1)S(1)}, u32[]{:S(2)}, u32[]{:S(2)}) collective-permute-start(bf16[128,256]{1,0:T(8,128)(2,1)S(1)} %get-tuple-element.90), channel_id=1, source_target_pairs={{0,24},{4,28},{8,16},{12,20},{16,8},{20,12},{24,0},{28,4},{1,25},{... | collective-permute-start | bytes 196616 | tf_op jit(solution)/shard_map/ppermute | solution.py:61
  107.2 4.4 %collective-permute-start.33 = (bf16[128,256]{1,0:T(8,128)(2,1)S(1)}, bf16[128,256]{1,0:T(8,128)(2,1)S(1)}, u32[]{:S(2)}, u32[]{:S(2)}) collective-permute-start(bf16[128,256]{1,0:T(8,128)(2,1)S(1)} %get-tuple-element.92), channel_id=1, source_target_pairs={{0,16},{4,20},{8,24},{12,28},{16,0},{20,4},{24,8},{28,12},{1,17},{... | collective-permute-start | bytes 196616 | tf_op jit(solution)/shard_map/ppermute | solution.py:61
  113.0 2.0 %collective-permute-start.36 = (bf16[128,256]{1,0:T(8,128)(2,1)S(1)}, bf16[128,256]{1,0:T(8,128)(2,1)S(1)}, u32[]{:S(2)}, u32[]{:S(2)}) collective-permute-start(bf16[128,256]{1,0:T(8,128)(2,1)S(1)} %get-tuple-element.95), channel_id=1, source_target_pairs={{0,4},{4,0},{8,12},{12,8},{16,20},{20,16},{24,28},{28,24},{1,5},{5... | collective-permute-start | bytes 196616 | tf_op jit(solution)/shard_map/ppermute | solution.py:61
  117.0 1.5 %collective-permute-done.34.refs_4_ = bf16[128,256]{1,0:T(8,128)(2,1)S(1)} collective-permute-done((bf16[128,256]{1,0:T(8,128)(2,1)S(1)}, bf16[128,256]{1,0:T(8,128)(2,1)S(1)}, u32[]{:S(2)}, u32[]{:S(2)}) %collective-permute-start.34) | collective-permute-done | bytes 65568 | tf_op jit(solution)/shard_map/ppermute | solution.py:61
  118.5 1.5 %combine_1.1 = bf16[512,256]{1,0:T(8,128)(2,1)} custom-call(s32[1]{0:T(128)} %bitcast.at_ref, s32[512,2]{1,0:T(8,128)S(1)} %get-tuple-element.51.targets_ref, f32[512,2]{1,0:T(8,128)S(1)} %copy.14.gates_ref, f32[512,256]{1,0:T(8,128)S(1)} %combine_0.1.base_ref, bf16[128,256]{1,0:T(8,128)(2,1)S(1)} %collective-permute-done.30.refs_0_, ...), custom_call_target="tpu_custom_call" | custom-call | flops 536870912 | bytes 3145728 | tf_op jit(solution)/shard_map/combine_1/pallas_call | solution.py:497
  (86 shorter events, 23.5 us)
Async XLA Ops:
  1.1 10.4 %collective-permute-start = (bf16[2,256,256]{2,1,0:T(8,128)(2,1)S(1)}, bf16[2,256,256]{2,1,0:T(8,128)(2,1)S(1)}, u32[]{:S(2)}, u32[]{:S(2)}) collective-permute-start(bf16[2,256,256]{2,1,0:T(8,128)(2,1)S(1)} %pad_maximum_fusion), channel_id=1, source_target_pairs={{0,4},{4,8},{8,12},{12,16},{16,20},{20,24},{24,28},{1,5},{5,9},{9,... | collective-permute-start | bytes 786440 | tf_op jit(solution)/shard_map/ppermute | solution.py:36
  9.7 4.9 %collective-permute-start.3 = (bf16[256,512]{1,0:T(8,128)(2,1)S(1)}, bf16[256,512]{1,0:T(8,128)(2,1)S(1)}, u32[]{:S(2)}, u32[]{:S(2)}) collective-permute-start(bf16[256,512]{1,0:T(8,128)(2,1)S(1)} %get-tuple-element.61), channel_id=1, source_target_pairs={{0,1},{1,0},{2,3},{3,2},{4,5},{5,4},{6,7},{7,6},{8,9},{9,8},{10,11... | collective-permute-start | bytes 786440 | tf_op jit(solution)/shard_map/ppermute | solution.py:41
  14.7 6.4 %collective-permute-start.4 = (bf16[256,256]{1,0:T(8,128)(2,1)S(1)}, bf16[256,256]{1,0:T(8,128)(2,1)S(1)}, u32[]{:S(2)}, u32[]{:S(2)}) collective-permute-start(bf16[256,256]{1,0:T(8,128)(2,1)S(1)} %add_late.1), channel_id=1, source_target_pairs={{0,2},{1,3},{2,0},{3,1},{4,6},{5,7},{6,4},{7,5},{8,10},{9,11},{10,... | collective-permute-start | bytes 393224 | tf_op jit(solution)/shard_map/ppermute | solution.py:47
  16.3 7.2 %collective-permute-start.2 = (bf16[256,256]{1,0:T(8,128)(2,1)S(1)}, bf16[256,256]{1,0:T(8,128)(2,1)S(1)}, u32[]{:S(2)}, u32[]{:S(2)}) collective-permute-start(bf16[256,256]{1,0:T(8,128)(2,1)S(1)} %add_early.1), channel_id=1, source_target_pairs={{0,2},{1,3},{2,0},{3,1},{4,6},{5,7},{6,4},{7,5},{8,10},{9,11},{10,... | collective-permute-start | bytes 393224 | tf_op jit(solution)/shard_map/ppermute | solution.py:47
  24.0 10.7 %collective-permute-start.5 = (bf16[512,256]{1,0:T(8,128)(2,1)S(1)}, bf16[512,256]{1,0:T(8,128)(2,1)S(1)}, u32[]{:S(2)}, u32[]{:S(2)}) collective-permute-start(bf16[512,256]{1,0:T(8,128)(2,1)S(1)} %get-tuple-element.64.refs_0_.base_ref), channel_id=1, source_target_pairs={{0,2},{1,3},{2,0},{3,1},{4,6},{5,7},{6,4},{7,5},{8,10},{9,11},{10,... | collective-permute-start | bytes 786440 | tf_op jit(solution)/shard_map/ppermute | solution.py:47
  25.5 11.3 %collective-permute-start.10 = (bf16[128,256]{1,0:T(8,128)(2,1)S(1)}, bf16[128,256]{1,0:T(8,128)(2,1)S(1)}, u32[]{:S(2)}, u32[]{:S(2)}) collective-permute-start(bf16[128,256]{1,0:T(8,128)(2,1)S(1)} %get-tuple-element.70), channel_id=1, source_target_pairs={{0,20},{4,16},{8,28},{12,24},{16,4},{20,0},{24,12},{28,8},{1,21},{... | collective-permute-start | bytes 196616 | tf_op jit(solution)/shard_map/ppermute | solution.py:61
  30.0 8.1 %collective-permute-start.11 = (bf16[128,256]{1,0:T(8,128)(2,1)S(1)}, bf16[128,256]{1,0:T(8,128)(2,1)S(1)}, u32[]{:S(2)}, u32[]{:S(2)}) collective-permute-start(bf16[128,256]{1,0:T(8,128)(2,1)S(1)} %get-tuple-element.71), channel_id=1, source_target_pairs={{0,24},{4,28},{8,16},{12,20},{16,8},{20,12},{24,0},{28,4},{1,25},{... | collective-permute-start | bytes 196616 | tf_op jit(solution)/shard_map/ppermute | solution.py:61
  31.4 9.9 %collective-permute-start.12 = (bf16[128,256]{1,0:T(8,128)(2,1)S(1)}, bf16[128,256]{1,0:T(8,128)(2,1)S(1)}, u32[]{:S(2)}, u32[]{:S(2)}) collective-permute-start(bf16[128,256]{1,0:T(8,128)(2,1)S(1)} %get-tuple-element.72), channel_id=1, source_target_pairs={{0,28},{4,24},{8,20},{12,16},{16,12},{20,8},{24,4},{28,0},{1,29},{... | collective-permute-start | bytes 196616 | tf_op jit(solution)/shard_map/ppermute | solution.py:61
  34.7 6.6 %collective-permute-start.7 = (bf16[128,256]{1,0:T(8,128)(2,1)S(1)}, bf16[128,256]{1,0:T(8,128)(2,1)S(1)}, u32[]{:S(2)}, u32[]{:S(2)}) collective-permute-start(bf16[128,256]{1,0:T(8,128)(2,1)S(1)} %get-tuple-element.67), channel_id=1, source_target_pairs={{0,8},{4,12},{8,0},{12,4},{16,24},{20,28},{24,16},{28,20},{1,9},{5... | collective-permute-start | bytes 196616 | tf_op jit(solution)/shard_map/ppermute | solution.py:61
  34.7 6.6 %collective-permute-start.8 = (bf16[128,256]{1,0:T(8,128)(2,1)S(1)}, bf16[128,256]{1,0:T(8,128)(2,1)S(1)}, u32[]{:S(2)}, u32[]{:S(2)}) collective-permute-start(bf16[128,256]{1,0:T(8,128)(2,1)S(1)} %get-tuple-element.68), channel_id=1, source_target_pairs={{0,12},{4,8},{8,4},{12,0},{16,28},{20,24},{24,20},{28,16},{1,13},{... | collective-permute-start | bytes 196616 | tf_op jit(solution)/shard_map/ppermute | solution.py:61
  36.8 5.9 %collective-permute-start.9 = (bf16[128,256]{1,0:T(8,128)(2,1)S(1)}, bf16[128,256]{1,0:T(8,128)(2,1)S(1)}, u32[]{:S(2)}, u32[]{:S(2)}) collective-permute-start(bf16[128,256]{1,0:T(8,128)(2,1)S(1)} %get-tuple-element.69), channel_id=1, source_target_pairs={{0,16},{4,20},{8,24},{12,28},{16,0},{20,4},{24,8},{28,12},{1,17},{... | collective-permute-start | bytes 196616 | tf_op jit(solution)/shard_map/ppermute | solution.py:61
  38.1 4.6 %collective-permute-start.6 = (bf16[128,256]{1,0:T(8,128)(2,1)S(1)}, bf16[128,256]{1,0:T(8,128)(2,1)S(1)}, u32[]{:S(2)}, u32[]{:S(2)}) collective-permute-start(bf16[128,256]{1,0:T(8,128)(2,1)S(1)} %take.2), channel_id=1, source_target_pairs={{0,4},{4,0},{8,12},{12,8},{16,20},{20,16},{24,28},{28,24},{1,5},{5... | collective-permute-start | bytes 196616 | tf_op jit(solution)/shard_map/ppermute | solution.py:61
  42.8 11.4 %collective-permute-start.13 = (bf16[1024,256]{1,0:T(8,128)(2,1)S(1)}, bf16[1024,256]{1,0:T(8,128)(2,1)S(1)}, u32[]{:S(2)}, u32[]{:S(2)}) collective-permute-start(bf16[1024,256]{1,0:T(8,128)(2,1)S(1)} %join.1.refs_0_), channel_id=1, source_target_pairs={{0,2},{1,3},{2,0},{3,1},{4,6},{5,7},{6,4},{7,5},{8,10},{9,11},{10,... | collective-permute-start | bytes 1572872 | tf_op jit(solution)/shard_map/ppermute | solution.py:47
  44.0 29.0 %all-to-all-start = ((bf16[8,128,512]{2,1,0:T(8,128)(2,1)}), bf16[8,128,512]{2,1,0:T(8,128)(2,1)S(1)}, u32[]{:S(2)}, u32[]{:S(2)}) async-start(bf16[8,128,512]{2,1,0:T(8,128)(2,1)} %bitcast.8), calls=%async_computation | async-start | bytes 2097152 | tf_op jit(solution)/shard_map/all_to_all | solution.py:449
  47.8 7.2 %collective-permute-start.14 = (bf16[1024,256]{1,0:T(8,128)(2,1)S(1)}, bf16[1024,256]{1,0:T(8,128)(2,1)S(1)}, u32[]{:S(2)}, u32[]{:S(2)}) collective-permute-start(bf16[1024,256]{1,0:T(8,128)(2,1)S(1)} %join.1.refs_0_), channel_id=1, source_target_pairs={{0,1},{1,0},{2,3},{3,2},{4,5},{5,4},{6,7},{7,6},{8,9},{9,8},{10,11... | collective-permute-start | bytes 1572872 | tf_op jit(solution)/shard_map/ppermute | solution.py:41
  73.2 14.3 %collective-permute-start.18 = (bf16[1024,256]{1,0:T(8,128)(2,1)S(1)}, bf16[1024,256]{1,0:T(8,128)(2,1)S(1)}, u32[]{:S(2)}, u32[]{:S(2)}) collective-permute-start(bf16[1024,256]{1,0:T(8,128)(2,1)S(1)} %add_0.1.refs_0_.refs_5_), channel_id=1, source_target_pairs={{0,2},{1,3},{2,0},{3,1},{4,6},{5,7},{6,4},{7,5},{8,10},{9,11},{10,... | collective-permute-start | bytes 1572872 | tf_op jit(solution)/shard_map/ppermute | solution.py:47
  86.1 8.1 %collective-permute-start.28 = (bf16[1024,256]{1,0:T(8,128)(2,1)S(1)}, bf16[1024,256]{1,0:T(8,128)(2,1)S(1)}, u32[]{:S(2)}, u32[]{:S(2)}) collective-permute-start(bf16[1024,256]{1,0:T(8,128)(2,1)S(1)} %get-tuple-element.88), channel_id=1, source_target_pairs={{0,1},{1,0},{2,3},{3,2},{4,5},{5,4},{6,7},{7,6},{8,9},{9,8},{10,11... | collective-permute-start | bytes 1572872 | tf_op jit(solution)/shard_map/ppermute | solution.py:41
  87.6 16.0 %collective-permute-start.29 = (bf16[1024,256]{1,0:T(8,128)(2,1)S(1)}, bf16[1024,256]{1,0:T(8,128)(2,1)S(1)}, u32[]{:S(2)}, u32[]{:S(2)}) collective-permute-start(bf16[1024,256]{1,0:T(8,128)(2,1)S(1)} %add_1.1.refs_2_), channel_id=1, source_target_pairs={{0,2},{1,3},{2,0},{3,1},{4,6},{5,7},{6,4},{7,5},{8,10},{9,11},{10,... | collective-permute-start | bytes 1572872 | tf_op jit(solution)/shard_map/ppermute | solution.py:47
  89.6 7.7 %collective-permute-start.21 = (bf16[128,256]{1,0:T(8,128)(2,1)S(1)}, bf16[128,256]{1,0:T(8,128)(2,1)S(1)}, u32[]{:S(2)}, u32[]{:S(2)}) collective-permute-start(bf16[128,256]{1,0:T(8,128)(2,1)S(1)} %get-tuple-element.79), channel_id=1, source_target_pairs={{0,28},{4,24},{8,20},{12,16},{16,12},{20,8},{24,4},{28,0},{1,29},{... | collective-permute-start | bytes 196616 | tf_op jit(solution)/shard_map/ppermute | solution.py:61
  91.8 6.9 %collective-permute-start.22 = (bf16[128,256]{1,0:T(8,128)(2,1)S(1)}, bf16[128,256]{1,0:T(8,128)(2,1)S(1)}, u32[]{:S(2)}, u32[]{:S(2)}) collective-permute-start(bf16[128,256]{1,0:T(8,128)(2,1)S(1)} %get-tuple-element.80), channel_id=1, source_target_pairs={{0,24},{4,28},{8,16},{12,20},{16,8},{20,12},{24,0},{28,4},{1,25},{... | collective-permute-start | bytes 196616 | tf_op jit(solution)/shard_map/ppermute | solution.py:61
  94.2 7.3 %collective-permute-start.23 = (bf16[128,256]{1,0:T(8,128)(2,1)S(1)}, bf16[128,256]{1,0:T(8,128)(2,1)S(1)}, u32[]{:S(2)}, u32[]{:S(2)}) collective-permute-start(bf16[128,256]{1,0:T(8,128)(2,1)S(1)} %get-tuple-element.81), channel_id=1, source_target_pairs={{0,20},{4,16},{8,28},{12,24},{16,4},{20,0},{24,12},{28,8},{1,21},{... | collective-permute-start | bytes 196616 | tf_op jit(solution)/shard_map/ppermute | solution.py:61
  94.2 11.0 %collective-permute-start.24 = (bf16[128,256]{1,0:T(8,128)(2,1)S(1)}, bf16[128,256]{1,0:T(8,128)(2,1)S(1)}, u32[]{:S(2)}, u32[]{:S(2)}) collective-permute-start(bf16[128,256]{1,0:T(8,128)(2,1)S(1)} %get-tuple-element.82), channel_id=1, source_target_pairs={{0,16},{4,20},{8,24},{12,28},{16,0},{20,4},{24,8},{28,12},{1,17},{... | collective-permute-start | bytes 196616 | tf_op jit(solution)/shard_map/ppermute | solution.py:61
  97.4 9.8 %collective-permute-start.25 = (bf16[128,256]{1,0:T(8,128)(2,1)S(1)}, bf16[128,256]{1,0:T(8,128)(2,1)S(1)}, u32[]{:S(2)}, u32[]{:S(2)}) collective-permute-start(bf16[128,256]{1,0:T(8,128)(2,1)S(1)} %get-tuple-element.83), channel_id=1, source_target_pairs={{0,12},{4,8},{8,4},{12,0},{16,28},{20,24},{24,20},{28,16},{1,13},{... | collective-permute-start | bytes 196616 | tf_op jit(solution)/shard_map/ppermute | solution.py:61
  98.7 8.4 %collective-permute-start.26 = (bf16[128,256]{1,0:T(8,128)(2,1)S(1)}, bf16[128,256]{1,0:T(8,128)(2,1)S(1)}, u32[]{:S(2)}, u32[]{:S(2)}) collective-permute-start(bf16[128,256]{1,0:T(8,128)(2,1)S(1)} %get-tuple-element.84), channel_id=1, source_target_pairs={{0,8},{4,12},{8,0},{12,4},{16,24},{20,28},{24,16},{28,20},{1,9},{5... | collective-permute-start | bytes 196616 | tf_op jit(solution)/shard_map/ppermute | solution.py:61
  101.4 10.1 %collective-permute-start.27 = (bf16[128,256]{1,0:T(8,128)(2,1)S(1)}, bf16[128,256]{1,0:T(8,128)(2,1)S(1)}, u32[]{:S(2)}, u32[]{:S(2)}) collective-permute-start(bf16[128,256]{1,0:T(8,128)(2,1)S(1)} %get-tuple-element.85), channel_id=1, source_target_pairs={{0,4},{4,0},{8,12},{12,8},{16,20},{20,16},{24,28},{28,24},{1,5},{5... | collective-permute-start | bytes 196616 | tf_op jit(solution)/shard_map/ppermute | solution.py:61
  103.8 7.8 %collective-permute-start.30 = (bf16[128,256]{1,0:T(8,128)(2,1)S(1)}, bf16[128,256]{1,0:T(8,128)(2,1)S(1)}, u32[]{:S(2)}, u32[]{:S(2)}) collective-permute-start(bf16[128,256]{1,0:T(8,128)(2,1)S(1)} %get-tuple-element.89), channel_id=1, source_target_pairs={{0,28},{4,24},{8,20},{12,16},{16,12},{20,8},{24,4},{28,0},{1,29},{... | collective-permute-start | bytes 196616 | tf_op jit(solution)/shard_map/ppermute | solution.py:61
  105.2 7.8 %collective-permute-start.31 = (bf16[128,256]{1,0:T(8,128)(2,1)S(1)}, bf16[128,256]{1,0:T(8,128)(2,1)S(1)}, u32[]{:S(2)}, u32[]{:S(2)}) collective-permute-start(bf16[128,256]{1,0:T(8,128)(2,1)S(1)} %get-tuple-element.90), channel_id=1, source_target_pairs={{0,24},{4,28},{8,16},{12,20},{16,8},{20,12},{24,0},{28,4},{1,25},{... | collective-permute-start | bytes 196616 | tf_op jit(solution)/shard_map/ppermute | solution.py:61
  107.2 9.8 %collective-permute-start.32 = (bf16[128,256]{1,0:T(8,128)(2,1)S(1)}, bf16[128,256]{1,0:T(8,128)(2,1)S(1)}, u32[]{:S(2)}, u32[]{:S(2)}) collective-permute-start(bf16[128,256]{1,0:T(8,128)(2,1)S(1)} %get-tuple-element.91), channel_id=1, source_target_pairs={{0,20},{4,16},{8,28},{12,24},{16,4},{20,0},{24,12},{28,8},{1,21},{... | collective-permute-start | bytes 196616 | tf_op jit(solution)/shard_map/ppermute | solution.py:61
  107.2 9.8 %collective-permute-start.33 = (bf16[128,256]{1,0:T(8,128)(2,1)S(1)}, bf16[128,256]{1,0:T(8,128)(2,1)S(1)}, u32[]{:S(2)}, u32[]{:S(2)}) collective-permute-start(bf16[128,256]{1,0:T(8,128)(2,1)S(1)} %get-tuple-element.92), channel_id=1, source_target_pairs={{0,16},{4,20},{8,24},{12,28},{16,0},{20,4},{24,8},{28,12},{1,17},{... | collective-permute-start | bytes 196616 | tf_op jit(solution)/shard_map/ppermute | solution.py:61
  111.5 6.9 %collective-permute-start.34 = (bf16[128,256]{1,0:T(8,128)(2,1)S(1)}, bf16[128,256]{1,0:T(8,128)(2,1)S(1)}, u32[]{:S(2)}, u32[]{:S(2)}) collective-permute-start(bf16[128,256]{1,0:T(8,128)(2,1)S(1)} %get-tuple-element.93), channel_id=1, source_target_pairs={{0,12},{4,8},{8,4},{12,0},{16,28},{20,24},{24,20},{28,16},{1,13},{... | collective-permute-start | bytes 196616 | tf_op jit(solution)/shard_map/ppermute | solution.py:61
  111.6 6.8 %collective-permute-start.35 = (bf16[128,256]{1,0:T(8,128)(2,1)S(1)}, bf16[128,256]{1,0:T(8,128)(2,1)S(1)}, u32[]{:S(2)}, u32[]{:S(2)}) collective-permute-start(bf16[128,256]{1,0:T(8,128)(2,1)S(1)} %get-tuple-element.94), channel_id=1, source_target_pairs={{0,8},{4,12},{8,0},{12,4},{16,24},{20,28},{24,16},{28,20},{1,9},{5... | collective-permute-start | bytes 196616 | tf_op jit(solution)/shard_map/ppermute | solution.py:61
  113.0 5.4 %collective-permute-start.36 = (bf16[128,256]{1,0:T(8,128)(2,1)S(1)}, bf16[128,256]{1,0:T(8,128)(2,1)S(1)}, u32[]{:S(2)}, u32[]{:S(2)}) collective-permute-start(bf16[128,256]{1,0:T(8,128)(2,1)S(1)} %get-tuple-element.95), channel_id=1, source_target_pairs={{0,4},{4,0},{8,12},{12,8},{16,20},{20,16},{24,28},{28,24},{1,5},{5... | collective-permute-start | bytes 196616 | tf_op jit(solution)/shard_map/ppermute | solution.py:61
  (15 other events, 118.9 us)
where the time goes:
time: 120 us
  starting transfers between devices  55.5 us (46%)
  Pallas kernels  32 us (27%)
  waiting for transfers between devices  26.8 us (22%)
  local copies, waits for them, and re-layouts  5.21 us (4%)
    ppermute x21, starting transfers between devices, exchanged(): moved[s] = lax.ppermute(blocks[s], 'tm', [(i, i ^ s) for i in range(size)])  36.4 us
    pallas_call x2, Pallas kernels, experts(): pl.pallas_call(functools.partial(expert_kernel, local, (0,) * len(parts),...  19.3 us
    ppermute x6, waiting for transfers between devices, from_chip(): return lax.ppermute(x, 'mp', pairs)  12.3 us
    ppermute x6, starting transfers between devices, from_chip(): return lax.ppermute(x, 'mp', pairs)  9.34 us
    ppermute x21, waiting for transfers between devices, exchanged(): moved[s] = lax.ppermute(blocks[s], 'tm', [(i, i ^ s) for i in range(size)])  5.78 us
    ppermute x1, starting transfers between devices, from_behind(): return lax.ppermute(x, axis, pairs)  4.89 us
    unnamed x20, local copies, waits for them, and re-layouts  4.08 us
    all_to_all x1, starting transfers between devices, over_time(): x = lax.all_to_all(x, 'tm', split_axis=0, concat_axis=0, tiled=True)  3.78 us
  transfers between devices with their start and end apart: 38, of which 14 were waited for; matrix products, arithmetic and copies ran while one was open for 0% of the time, Pallas kernels for 25%

commit v1 on v0

--- a/solution.py
+++ b/solution.py
@@ -96,15 +96,9 @@
             (proj_any, proj_ref),
         ]
     else:
-        edges_ref, q_all, k_all, v_all, proj_ref, tails_any = refs[:6]
-        send_ref, keep_x_ref, keep_ref, k_ref, v_ref, sems = refs[6:]
-        first_rows = pl.ds(0, keep_ref.shape[0])
-        moves = [
-            (tails_any.at[0], k_ref.at[pl.ds(0, LEFT)]),
-            (k_all.at[first_rows], k_ref.at[pl.ds(LEFT, keep_ref.shape[0])]),
-            (tails_any.at[1], v_ref.at[pl.ds(0, LEFT)]),
-            (v_all.at[first_rows], v_ref.at[pl.ds(LEFT, keep_ref.shape[0])]),
-        ]
+        edges_ref, q_all, k_ref, v_ref, proj_ref, tails_ref = refs[:6]
+        send_ref, keep_x_ref, keep_ref = refs[6:]
+        moves = []
     rows, columns = keep_ref.shape
     heads = columns // head_width
     block = LANES
@@ -119,8 +113,12 @@
     lane_head = lax.broadcasted_iota(jnp.int32, (block, columns), 1) // head_width
     context = []
     for r in range(0, rows, block):
-        key = k_ref[r : r + window, :]
-        value = v_ref[r : r + window, :]
+        if start > 0:
+            key = k_ref[start - LEFT + r : start + r + block, :]
+            value = v_ref[start - LEFT + r : start + r + block, :]
+        else:
+            key = jnp.concatenate([tails_ref[0, r:LEFT, :], k_ref[0 : r + block, :]], 0)
+            value = jnp.concatenate([tails_ref[1, r:LEFT, :], v_ref[0 : r + block, :]], 0)
         query = q_all[start + r : start + r + block, :]
         places = lax.broadcasted_iota(jnp.int32, (block, window), 1)
         places = (places + (meta_ref[0] + (start + r - LEFT))).astype(F32)
@@ -387,13 +385,8 @@
     early = pl.pallas_call(
         functools.partial(attend_kernel, scale, head_width, 0),
         out_shape=attended_outs(LEFT),
-        in_specs=[SMEM, SMEM] + [VMEM] * 5 + [ANY],
+        in_specs=[SMEM, SMEM] + [VMEM] * 6,
         out_specs=(VMEM,) * 3,
-        scratch_shapes=[
-            pltpu.VMEM((2 * LEFT, width), BF16),
-            pltpu.VMEM((2 * LEFT, width), BF16),
-            pltpu.SemaphoreType.DMA((4,)),
-        ],
         compiler_params=params(16),
         cost_estimate=attend_cost(LEFT),
         name="attend_early",

time: 120 us -> 120 us (level)
  transfers between devices with their start and end apart: 38 -> 38, of which waited for: 14 -> 14; matrix products, arithmetic and copies ran while one was open for 0% -> 0% of each run, Pallas kernels for 25% -> 24%
where the time goes in v1:
time: 120 us; the launch traced here: 119 us
  starting transfers between devices  55.5 us (46%)
  Pallas kernels  31.3 us (26%)
  waiting for transfers between devices  26.8 us (22%)
  local copies, waits for them, and re-layouts  5.21 us (4%)
    ppermute x21, starting transfers between devices, exchanged(): moved[s] = lax.ppermute(blocks[s], 'tm', [(i, i ^ s) for i in range(size)])  36.4 us
    pallas_call x2, Pallas kernels, experts(): pl.pallas_call(functools.partial(expert_kernel, local, (0,) * len(parts),...  19.3 us
    ppermute x6, waiting for transfers between devices, from_chip(): return lax.ppermute(x, 'mp', pairs)  12.3 us
    ppermute x6, starting transfers between devices, from_chip(): return lax.ppermute(x, 'mp', pairs)  9.33 us
    ppermute x21, waiting for transfers between devices, exchanged(): moved[s] = lax.ppermute(blocks[s], 'tm', [(i, i ^ s) for i in range(size)])  5.78 us
    ppermute x1, starting transfers between devices, from_behind(): return lax.ppermute(x, axis, pairs)  4.89 us
    unnamed x20, local copies, waits for them, and re-layouts  4.08 us
    all_to_all x1, starting transfers between devices, over_time(): x = lax.all_to_all(x, 'tm', split_axis=0, concat_axis=0, tiled=True)  3.78 us
  transfers between devices with their start and end apart: 38, of which 14 were waited for; matrix products, arithmetic and copies ran while one was open for 0% of the time, Pallas kernels for 24%

profile of v1, /device:TPU:0, one launch (start us, length us, event | category | flops | bytes accessed | tf_op | source)
XLA Modules:
  0.0 119.3 jit_solution(13017855083638802148)
XLA Ops:
  1.1 4.9 %collective-permute-start = (bf16[2,256,256]{2,1,0:T(8,128)(2,1)S(1)}, bf16[2,256,256]{2,1,0:T(8,128)(2,1)S(1)}, u32[]{:S(2)}, u32[]{:S(2)}) collective-permute-start(bf16[2,256,256]{2,1,0:T(8,128)(2,1)S(1)} %pad_maximum_fusion), channel_id=1, source_target_pairs={{0,4},{4,8},{8,12},{12,16},{16,20},{20,24},{24,28},{1,5},{5,9},{9,... | collective-permute-start | bytes 786440 | tf_op jit(solution)/shard_map/ppermute | solution.py:36
  6.2 3.5 %attend_late.1 = (bf16[256,512]{1,0:T(8,128)(2,1)S(1)}, f32[256,256]{1,0:T(8,128)S(1)}, f32[256,256]{1,0:T(8,128)S(1)}, s32[2,512]{1,0:T(2,128)S(1)}, bf16[512,2...) custom-call(s32[1]{0:T(128)} %bitcast.1.meta_ref, ...), custom_call_target="tpu_custom_call" | custom-call | flops 402653184 | bytes 524288 | tf_op jit(solution)/shard_map/attend_late/pallas_call | solution.py:374
  9.8 1.8 %collective-permute-done.refs_5_ = bf16[2,256,256]{2,1,0:T(8,128)(2,1)S(1)} collective-permute-done((bf16[2,256,256]{2,1,0:T(8,128)(2,1)S(1)}, bf16[2,256,256]{2,1,0:T(8,128)(2,1)S(1)}, u32[]{:S(2)}, u32[]{:S(2)}) %collective-permute-start) | collective-permute-done | bytes 262176 | tf_op jit(solution)/shard_map/ppermute | solution.py:36
  11.6 2.3 %attend_early.1 = (bf16[256,512]{1,0:T(8,128)(2,1)S(1)}, f32[256,256]{1,0:T(8,128)S(1)}, f32[256,256]{1,0:T(8,128)S(1)}) custom-call(s32[1]{0:T(128)} %bitcast.1.meta_ref, s32[4]{0:T(128)S(1)} %pad_add_fusion.order_ref, s32[2,512]{1,0:T(2,128)S(1)} %get-tuple-element.52.refs_0_, bf16[512,256]{1,0:T(8,128)(2,1)S(1)} %get-tuple-element.53.refs_1_, ...), custom_call_target="tpu_custom_call" | custom-call | flops 402653184 | bytes 524288 | tf_op jit(solution)/shard_map/attend_early/pallas_call | solution.py:385
  14.0 1.5 %collective-permute-start.4 = (bf16[256,256]{1,0:T(8,128)(2,1)S(1)}, bf16[256,256]{1,0:T(8,128)(2,1)S(1)}, u32[]{:S(2)}, u32[]{:S(2)}) collective-permute-start(bf16[256,256]{1,0:T(8,128)(2,1)S(1)} %add_late.1), channel_id=1, source_target_pairs={{0,2},{1,3},{2,0},{3,1},{4,6},{5,7},{6,4},{7,5},{8,10},{9,11},{10,... | collective-permute-start | bytes 393224 | tf_op jit(solution)/shard_map/ppermute | solution.py:47
  15.5 1.5 %collective-permute-start.2 = (bf16[256,256]{1,0:T(8,128)(2,1)S(1)}, bf16[256,256]{1,0:T(8,128)(2,1)S(1)}, u32[]{:S(2)}, u32[]{:S(2)}) collective-permute-start(bf16[256,256]{1,0:T(8,128)(2,1)S(1)} %add_early.1), channel_id=1, source_target_pairs={{0,2},{1,3},{2,0},{3,1},{4,6},{5,7},{6,4},{7,5},{8,10},{9,11},{10,... | collective-permute-start | bytes 393224 | tf_op jit(solution)/shard_map/ppermute | solution.py:47
  18.1 2.2 %collective-permute-done.4.refs_5_ = bf16[256,256]{1,0:T(8,128)(2,1)S(1)} collective-permute-done((bf16[256,256]{1,0:T(8,128)(2,1)S(1)}, bf16[256,256]{1,0:T(8,128)(2,1)S(1)}, u32[]{:S(2)}, u32[]{:S(2)}) %collective-permute-start.4) | collective-permute-done | bytes 131104 | tf_op jit(solution)/shard_map/ppermute | solution.py:47
  20.3 2.4 %collective-permute-done.2.refs_2_ = bf16[256,256]{1,0:T(8,128)(2,1)S(1)} collective-permute-done((bf16[256,256]{1,0:T(8,128)(2,1)S(1)}, bf16[256,256]{1,0:T(8,128)(2,1)S(1)}, u32[]{:S(2)}, u32[]{:S(2)}) %collective-permute-start.2) | collective-permute-done | bytes 131104 | tf_op jit(solution)/shard_map/ppermute | solution.py:47
  23.3 1.5 %collective-permute-start.5 = (bf16[512,256]{1,0:T(8,128)(2,1)S(1)}, bf16[512,256]{1,0:T(8,128)(2,1)S(1)}, u32[]{:S(2)}, u32[]{:S(2)}) collective-permute-start(bf16[512,256]{1,0:T(8,128)(2,1)S(1)} %get-tuple-element.64.refs_0_.base_ref), channel_id=1, source_target_pairs={{0,2},{1,3},{2,0},{3,1},{4,6},{5,7},{6,4},{7,5},{8,10},{9,11},{10,... | collective-permute-start | bytes 786440 | tf_op jit(solution)/shard_map/ppermute | solution.py:47
  24.8 4.5 %collective-permute-start.10 = (bf16[128,256]{1,0:T(8,128)(2,1)S(1)}, bf16[128,256]{1,0:T(8,128)(2,1)S(1)}, u32[]{:S(2)}, u32[]{:S(2)}) collective-permute-start(bf16[128,256]{1,0:T(8,128)(2,1)S(1)} %get-tuple-element.70), channel_id=1, source_target_pairs={{0,20},{4,16},{8,28},{12,24},{16,4},{20,0},{24,12},{28,8},{1,21},{... | collective-permute-start | bytes 196616 | tf_op jit(solution)/shard_map/ppermute | solution.py:61
  30.7 3.3 %collective-permute-start.12 = (bf16[128,256]{1,0:T(8,128)(2,1)S(1)}, bf16[128,256]{1,0:T(8,128)(2,1)S(1)}, u32[]{:S(2)}, u32[]{:S(2)}) collective-permute-start(bf16[128,256]{1,0:T(8,128)(2,1)S(1)} %get-tuple-element.72), channel_id=1, source_target_pairs={{0,28},{4,24},{8,20},{12,16},{16,12},{20,8},{24,4},{28,0},{1,29},{... | collective-permute-start | bytes 196616 | tf_op jit(solution)/shard_map/ppermute | solution.py:61
  34.0 2.1 %collective-permute-start.8 = (bf16[128,256]{1,0:T(8,128)(2,1)S(1)}, bf16[128,256]{1,0:T(8,128)(2,1)S(1)}, u32[]{:S(2)}, u32[]{:S(2)}) collective-permute-start(bf16[128,256]{1,0:T(8,128)(2,1)S(1)} %get-tuple-element.68), channel_id=1, source_target_pairs={{0,12},{4,8},{8,4},{12,0},{16,28},{20,24},{24,20},{28,16},{1,13},{... | collective-permute-start | bytes 196616 | tf_op jit(solution)/shard_map/ppermute | solution.py:61
  37.4 1.4 %collective-permute-start.6 = (bf16[128,256]{1,0:T(8,128)(2,1)S(1)}, bf16[128,256]{1,0:T(8,128)(2,1)S(1)}, u32[]{:S(2)}, u32[]{:S(2)}) collective-permute-start(bf16[128,256]{1,0:T(8,128)(2,1)S(1)} %take.2), channel_id=1, source_target_pairs={{0,4},{4,0},{8,12},{12,8},{16,20},{20,16},{24,28},{28,24},{1,5},{5... | collective-permute-start | bytes 196616 | tf_op jit(solution)/shard_map/ppermute | solution.py:61
  38.8 1.7 %dispatch.1.refs_8_.refs_7_ = bf16[1024,512]{1,0:T(8,128)(2,1)} custom-call(bf16[512,256]{1,0:T(8,128)(2,1)S(1)} %get-tuple-element.64.refs_0_.base_ref, bf16[512,256]{1,0:T(8,128)(2,1)S(1)} %collective-permute-done.5.refs_0_.refs_1_, f32[128,512]{1,0:T(8,128)S(1)} %get-tuple-element.63.refs_7_.refs_2_), custom_call_target="tpu_custom_call" | custom-call | flops 536870912 | bytes 3145728 | tf_op jit(solution)/shard_map/dispatch/pallas_call | solution.py:429
  40.6 1.4 %collective-permute-done.9.refs_4_ = bf16[128,256]{1,0:T(8,128)(2,1)S(1)} collective-permute-done((bf16[128,256]{1,0:T(8,128)(2,1)S(1)}, bf16[128,256]{1,0:T(8,128)(2,1)S(1)}, u32[]{:S(2)}, u32[]{:S(2)}) %collective-permute-start.9) | collective-permute-done | bytes 65568 | tf_op jit(solution)/shard_map/ppermute | solution.py:61
  43.3 3.8 %all-to-all-start = ((bf16[8,128,512]{2,1,0:T(8,128)(2,1)}), bf16[8,128,512]{2,1,0:T(8,128)(2,1)S(1)}, u32[]{:S(2)}, u32[]{:S(2)}) async-start(bf16[8,128,512]{2,1,0:T(8,128)(2,1)} %bitcast.8), calls=%async_computation | async-start | bytes 2097152 | tf_op jit(solution)/shard_map/all_to_all | solution.py:442
  47.1 6.4 %collective-permute-done.13.refs_1_ = bf16[1024,256]{1,0:T(8,128)(2,1)S(1)} collective-permute-done((bf16[1024,256]{1,0:T(8,128)(2,1)S(1)}, bf16[1024,256]{1,0:T(8,128)(2,1)S(1)}, u32[]{:S(2)}, u32[]{:S(2)}) %collective-permute-start.13) | collective-permute-done | bytes 524320 | tf_op jit(solution)/shard_map/ppermute | solution.py:47
  56.4 9.7 %experts_0.1 = (bf16[1024,256]{1,0:T(8,128)(2,1)S(1)}, bf16[1024,256]{1,0:T(8,128)(2,1)S(1)}, f32[1024,256]{1,0:T(8,128)S(1)}, f32[1024,256]{1,0:T(8,128)S(1)}) custom-call(s32[4]{0:T(128)S(1)} %pad_add_fusion.order_ref, bf16[1024,256]{1,0:T(8,128)(2,1)S(1)} %join.1.refs_0_, bf16[1024,256]{1,0:T(8,128)(2,1)S(1)} %copy-done.4, ...), custom_call_target="tpu_custom_call" | custom-call | flops 6442450944 | bytes 12582912 | tf_op jit(solution)/shard_map/experts_0/pallas_call | solution.py:459
  67.2 1.8 %collective-permute-done.17.got_ref = bf16[1024,256]{1,0:T(8,128)(2,1)S(1)} collective-permute-done((bf16[1024,256]{1,0:T(8,128)(2,1)S(1)}, bf16[1024,256]{1,0:T(8,128)(2,1)S(1)}, u32[]{:S(2)}, u32[]{:S(2)}) %collective-permute-start.17) | collective-permute-done | bytes 524320 | tf_op jit(solution)/shard_map/ppermute | solution.py:41
  69.1 3.2 %all-to-all-done = bf16[8,128,512]{2,1,0:T(8,128)(2,1)S(1)} async-done(((bf16[8,128,512]{2,1,0:T(8,128)(2,1)}), bf16[8,128,512]{2,1,0:T(8,128)(2,1)S(1)}, u32[]{:S(2)}, u32[]{:S(2)}) %all-to-all-start) | async-done | bytes 1048608 | tf_op jit(solution)/shard_map/all_to_all | solution.py:442
  72.5 1.8 %collective-permute-start.18 = (bf16[1024,256]{1,0:T(8,128)(2,1)S(1)}, bf16[1024,256]{1,0:T(8,128)(2,1)S(1)}, u32[]{:S(2)}, u32[]{:S(2)}) collective-permute-start(bf16[1024,256]{1,0:T(8,128)(2,1)S(1)} %add_0.1.refs_0_.refs_5_), channel_id=1, source_target_pairs={{0,2},{1,3},{2,0},{3,1},{4,6},{5,7},{6,4},{7,5},{8,10},{9,11},{10,... | collective-permute-start | bytes 1572872 | tf_op jit(solution)/shard_map/ppermute | solution.py:47
  75.1 9.7 %experts_1.1 = (bf16[1024,256]{1,0:T(8,128)(2,1)S(1)}, bf16[1024,256]{1,0:T(8,128)(2,1)S(1)}, f32[1024,256]{1,0:T(8,128)S(1)}, f32[1024,256]{1,0:T(8,128)S(1)}) custom-call(s32[4]{0:T(128)S(1)} %pad_add_fusion.order_ref, bf16[1024,512]{1,0:T(8,128)(2,1)S(1)} %take.3.refs_0_, bf16[1024,512]{1,0:T(8,128)(2,1)S(1)} %collective-permute-done.19.refs_1_, ...), custom_call_target="tpu_custom_call" | custom-call | flops 6442450944 | bytes 12582912 | tf_op jit(solution)/shard_map/experts_1/pallas_call | solution.py:459
  86.9 1.8 %collective-permute-start.29 = (bf16[1024,256]{1,0:T(8,128)(2,1)S(1)}, bf16[1024,256]{1,0:T(8,128)(2,1)S(1)}, u32[]{:S(2)}, u32[]{:S(2)}) collective-permute-start(bf16[1024,256]{1,0:T(8,128)(2,1)S(1)} %add_1.1.refs_2_), channel_id=1, source_target_pairs={{0,2},{1,3},{2,0},{3,1},{4,6},{5,7},{6,4},{7,5},{8,10},{9,11},{10,... | collective-permute-start | bytes 1572872 | tf_op jit(solution)/shard_map/ppermute | solution.py:47
  88.9 2.2 %collective-permute-start.21 = (bf16[128,256]{1,0:T(8,128)(2,1)S(1)}, bf16[128,256]{1,0:T(8,128)(2,1)S(1)}, u32[]{:S(2)}, u32[]{:S(2)}) collective-permute-start(bf16[128,256]{1,0:T(8,128)(2,1)S(1)} %get-tuple-element.79), channel_id=1, source_target_pairs={{0,28},{4,24},{8,20},{12,16},{16,12},{20,8},{24,4},{28,0},{1,29},{... | collective-permute-start | bytes 196616 | tf_op jit(solution)/shard_map/ppermute | solution.py:61
  91.1 2.4 %collective-permute-start.22 = (bf16[128,256]{1,0:T(8,128)(2,1)S(1)}, bf16[128,256]{1,0:T(8,128)(2,1)S(1)}, u32[]{:S(2)}, u32[]{:S(2)}) collective-permute-start(bf16[128,256]{1,0:T(8,128)(2,1)S(1)} %get-tuple-element.80), channel_id=1, source_target_pairs={{0,24},{4,28},{8,16},{12,20},{16,8},{20,12},{24,0},{28,4},{1,25},{... | collective-permute-start | bytes 196616 | tf_op jit(solution)/shard_map/ppermute | solution.py:61
  93.5 3.2 %collective-permute-start.24 = (bf16[128,256]{1,0:T(8,128)(2,1)S(1)}, bf16[128,256]{1,0:T(8,128)(2,1)S(1)}, u32[]{:S(2)}, u32[]{:S(2)}) collective-permute-start(bf16[128,256]{1,0:T(8,128)(2,1)S(1)} %get-tuple-element.82), channel_id=1, source_target_pairs={{0,16},{4,20},{8,24},{12,28},{16,0},{20,4},{24,8},{28,12},{1,17},{... | collective-permute-start | bytes 196616 | tf_op jit(solution)/shard_map/ppermute | solution.py:61
  100.7 2.2 %collective-permute-start.27 = (bf16[128,256]{1,0:T(8,128)(2,1)S(1)}, bf16[128,256]{1,0:T(8,128)(2,1)S(1)}, u32[]{:S(2)}, u32[]{:S(2)}) collective-permute-start(bf16[128,256]{1,0:T(8,128)(2,1)S(1)} %get-tuple-element.85), channel_id=1, source_target_pairs={{0,4},{4,0},{8,12},{12,8},{16,20},{20,16},{24,28},{28,24},{1,5},{5... | collective-permute-start | bytes 196616 | tf_op jit(solution)/shard_map/ppermute | solution.py:61
  104.5 2.0 %collective-permute-start.31 = (bf16[128,256]{1,0:T(8,128)(2,1)S(1)}, bf16[128,256]{1,0:T(8,128)(2,1)S(1)}, u32[]{:S(2)}, u32[]{:S(2)}) collective-permute-start(bf16[128,256]{1,0:T(8,128)(2,1)S(1)} %get-tuple-element.90), channel_id=1, source_target_pairs={{0,24},{4,28},{8,16},{12,20},{16,8},{20,12},{24,0},{28,4},{1,25},{... | collective-permute-start | bytes 196616 | tf_op jit(solution)/shard_map/ppermute | solution.py:61
  106.4 4.4 %collective-permute-start.33 = (bf16[128,256]{1,0:T(8,128)(2,1)S(1)}, bf16[128,256]{1,0:T(8,128)(2,1)S(1)}, u32[]{:S(2)}, u32[]{:S(2)}) collective-permute-start(bf16[128,256]{1,0:T(8,128)(2,1)S(1)} %get-tuple-element.92), channel_id=1, source_target_pairs={{0,16},{4,20},{8,24},{12,28},{16,0},{20,4},{24,8},{28,12},{1,17},{... | collective-permute-start | bytes 196616 | tf_op jit(solution)/shard_map/ppermute | solution.py:61
  112.3 2.0 %collective-permute-start.36 = (bf16[128,256]{1,0:T(8,128)(2,1)S(1)}, bf16[128,256]{1,0:T(8,128)(2,1)S(1)}, u32[]{:S(2)}, u32[]{:S(2)}) collective-permute-start(bf16[128,256]{1,0:T(8,128)(2,1)S(1)} %get-tuple-element.95), channel_id=1, source_target_pairs={{0,4},{4,0},{8,12},{12,8},{16,20},{20,16},{24,28},{28,24},{1,5},{5... | collective-permute-start | bytes 196616 | tf_op jit(solution)/shard_map/ppermute | solution.py:61
  116.3 1.5 %collective-permute-done.34.refs_4_ = bf16[128,256]{1,0:T(8,128)(2,1)S(1)} collective-permute-done((bf16[128,256]{1,0:T(8,128)(2,1)S(1)}, bf16[128,256]{1,0:T(8,128)(2,1)S(1)}, u32[]{:S(2)}, u32[]{:S(2)}) %collective-permute-start.34) | collective-permute-done | bytes 65568 | tf_op jit(solution)/shard_map/ppermute | solution.py:61
  117.8 1.5 %combine_1.1 = bf16[512,256]{1,0:T(8,128)(2,1)} custom-call(s32[1]{0:T(128)} %bitcast.at_ref, s32[512,2]{1,0:T(8,128)S(1)} %get-tuple-element.51.targets_ref, f32[512,2]{1,0:T(8,128)S(1)} %copy.14.gates_ref, f32[512,256]{1,0:T(8,128)S(1)} %combine_0.1.base_ref, bf16[128,256]{1,0:T(8,128)(2,1)S(1)} %collective-permute-done.30.refs_0_, ...), custom_call_target="tpu_custom_call" | custom-call | flops 536870912 | bytes 3145728 | tf_op jit(solution)/shard_map/combine_1/pallas_call | solution.py:490
  (86 shorter events, 23.5 us)
Async XLA Ops:
  1.1 10.4 %collective-permute-start = (bf16[2,256,256]{2,1,0:T(8,128)(2,1)S(1)}, bf16[2,256,256]{2,1,0:T(8,128)(2,1)S(1)}, u32[]{:S(2)}, u32[]{:S(2)}) collective-permute-start(bf16[2,256,256]{2,1,0:T(8,128)(2,1)S(1)} %pad_maximum_fusion), channel_id=1, source_target_pairs={{0,4},{4,8},{8,12},{12,16},{16,20},{20,24},{24,28},{1,5},{5,9},{9,... | collective-permute-start | bytes 786440 | tf_op jit(solution)/shard_map/ppermute | solution.py:36
  9.7 4.2 %collective-permute-start.3 = (bf16[256,512]{1,0:T(8,128)(2,1)S(1)}, bf16[256,512]{1,0:T(8,128)(2,1)S(1)}, u32[]{:S(2)}, u32[]{:S(2)}) collective-permute-start(bf16[256,512]{1,0:T(8,128)(2,1)S(1)} %get-tuple-element.61), channel_id=1, source_target_pairs={{0,1},{1,0},{2,3},{3,2},{4,5},{5,4},{6,7},{7,6},{8,9},{9,8},{10,11... | collective-permute-start | bytes 786440 | tf_op jit(solution)/shard_map/ppermute | solution.py:41
  14.0 6.4 %collective-permute-start.4 = (bf16[256,256]{1,0:T(8,128)(2,1)S(1)}, bf16[256,256]{1,0:T(8,128)(2,1)S(1)}, u32[]{:S(2)}, u32[]{:S(2)}) collective-permute-start(bf16[256,256]{1,0:T(8,128)(2,1)S(1)} %add_late.1), channel_id=1, source_target_pairs={{0,2},{1,3},{2,0},{3,1},{4,6},{5,7},{6,4},{7,5},{8,10},{9,11},{10,... | collective-permute-start | bytes 393224 | tf_op jit(solution)/shard_map/ppermute | solution.py:47
  15.5 7.2 %collective-permute-start.2 = (bf16[256,256]{1,0:T(8,128)(2,1)S(1)}, bf16[256,256]{1,0:T(8,128)(2,1)S(1)}, u32[]{:S(2)}, u32[]{:S(2)}) collective-permute-start(bf16[256,256]{1,0:T(8,128)(2,1)S(1)} %add_early.1), channel_id=1, source_target_pairs={{0,2},{1,3},{2,0},{3,1},{4,6},{5,7},{6,4},{7,5},{8,10},{9,11},{10,... | collective-permute-start | bytes 393224 | tf_op jit(solution)/shard_map/ppermute | solution.py:47
  23.3 10.7 %collective-permute-start.5 = (bf16[512,256]{1,0:T(8,128)(2,1)S(1)}, bf16[512,256]{1,0:T(8,128)(2,1)S(1)}, u32[]{:S(2)}, u32[]{:S(2)}) collective-permute-start(bf16[512,256]{1,0:T(8,128)(2,1)S(1)} %get-tuple-element.64.refs_0_.base_ref), channel_id=1, source_target_pairs={{0,2},{1,3},{2,0},{3,1},{4,6},{5,7},{6,4},{7,5},{8,10},{9,11},{10,... | collective-permute-start | bytes 786440 | tf_op jit(solution)/shard_map/ppermute | solution.py:47
  24.8 11.3 %collective-permute-start.10 = (bf16[128,256]{1,0:T(8,128)(2,1)S(1)}, bf16[128,256]{1,0:T(8,128)(2,1)S(1)}, u32[]{:S(2)}, u32[]{:S(2)}) collective-permute-start(bf16[128,256]{1,0:T(8,128)(2,1)S(1)} %get-tuple-element.70), channel_id=1, source_target_pairs={{0,20},{4,16},{8,28},{12,24},{16,4},{20,0},{24,12},{28,8},{1,21},{... | collective-permute-start | bytes 196616 | tf_op jit(solution)/shard_map/ppermute | solution.py:61
  29.3 8.1 %collective-permute-start.11 = (bf16[128,256]{1,0:T(8,128)(2,1)S(1)}, bf16[128,256]{1,0:T(8,128)(2,1)S(1)}, u32[]{:S(2)}, u32[]{:S(2)}) collective-permute-start(bf16[128,256]{1,0:T(8,128)(2,1)S(1)} %get-tuple-element.71), channel_id=1, source_target_pairs={{0,24},{4,28},{8,16},{12,20},{16,8},{20,12},{24,0},{28,4},{1,25},{... | collective-permute-start | bytes 196616 | tf_op jit(solution)/shard_map/ppermute | solution.py:61
  30.7 9.9 %collective-permute-start.12 = (bf16[128,256]{1,0:T(8,128)(2,1)S(1)}, bf16[128,256]{1,0:T(8,128)(2,1)S(1)}, u32[]{:S(2)}, u32[]{:S(2)}) collective-permute-start(bf16[128,256]{1,0:T(8,128)(2,1)S(1)} %get-tuple-element.72), channel_id=1, source_target_pairs={{0,28},{4,24},{8,20},{12,16},{16,12},{20,8},{24,4},{28,0},{1,29},{... | collective-permute-start | bytes 196616 | tf_op jit(solution)/shard_map/ppermute | solution.py:61
  34.0 6.6 %collective-permute-start.7 = (bf16[128,256]{1,0:T(8,128)(2,1)S(1)}, bf16[128,256]{1,0:T(8,128)(2,1)S(1)}, u32[]{:S(2)}, u32[]{:S(2)}) collective-permute-start(bf16[128,256]{1,0:T(8,128)(2,1)S(1)} %get-tuple-element.67), channel_id=1, source_target_pairs={{0,8},{4,12},{8,0},{12,4},{16,24},{20,28},{24,16},{28,20},{1,9},{5... | collective-permute-start | bytes 196616 | tf_op jit(solution)/shard_map/ppermute | solution.py:61
  34.0 6.6 %collective-permute-start.8 = (bf16[128,256]{1,0:T(8,128)(2,1)S(1)}, bf16[128,256]{1,0:T(8,128)(2,1)S(1)}, u32[]{:S(2)}, u32[]{:S(2)}) collective-permute-start(bf16[128,256]{1,0:T(8,128)(2,1)S(1)} %get-tuple-element.68), channel_id=1, source_target_pairs={{0,12},{4,8},{8,4},{12,0},{16,28},{20,24},{24,20},{28,16},{1,13},{... | collective-permute-start | bytes 196616 | tf_op jit(solution)/shard_map/ppermute | solution.py:61
  36.1 5.9 %collective-permute-start.9 = (bf16[128,256]{1,0:T(8,128)(2,1)S(1)}, bf16[128,256]{1,0:T(8,128)(2,1)S(1)}, u32[]{:S(2)}, u32[]{:S(2)}) collective-permute-start(bf16[128,256]{1,0:T(8,128)(2,1)S(1)} %get-tuple-element.69), channel_id=1, source_target_pairs={{0,16},{4,20},{8,24},{12,28},{16,0},{20,4},{24,8},{28,12},{1,17},{... | collective-permute-start | bytes 196616 | tf_op jit(solution)/shard_map/ppermute | solution.py:61
  37.4 4.6 %collective-permute-start.6 = (bf16[128,256]{1,0:T(8,128)(2,1)S(1)}, bf16[128,256]{1,0:T(8,128)(2,1)S(1)}, u32[]{:S(2)}, u32[]{:S(2)}) collective-permute-start(bf16[128,256]{1,0:T(8,128)(2,1)S(1)} %take.2), channel_id=1, source_target_pairs={{0,4},{4,0},{8,12},{12,8},{16,20},{20,16},{24,28},{28,24},{1,5},{5... | collective-permute-start | bytes 196616 | tf_op jit(solution)/shard_map/ppermute | solution.py:61
  42.0 11.4 %collective-permute-start.13 = (bf16[1024,256]{1,0:T(8,128)(2,1)S(1)}, bf16[1024,256]{1,0:T(8,128)(2,1)S(1)}, u32[]{:S(2)}, u32[]{:S(2)}) collective-permute-start(bf16[1024,256]{1,0:T(8,128)(2,1)S(1)} %join.1.refs_0_), channel_id=1, source_target_pairs={{0,2},{1,3},{2,0},{3,1},{4,6},{5,7},{6,4},{7,5},{8,10},{9,11},{10,... | collective-permute-start | bytes 1572872 | tf_op jit(solution)/shard_map/ppermute | solution.py:47
  43.3 29.0 %all-to-all-start = ((bf16[8,128,512]{2,1,0:T(8,128)(2,1)}), bf16[8,128,512]{2,1,0:T(8,128)(2,1)S(1)}, u32[]{:S(2)}, u32[]{:S(2)}) async-start(bf16[8,128,512]{2,1,0:T(8,128)(2,1)} %bitcast.8), calls=%async_computation | async-start | bytes 2097152 | tf_op jit(solution)/shard_map/all_to_all | solution.py:442
  47.0 7.2 %collective-permute-start.14 = (bf16[1024,256]{1,0:T(8,128)(2,1)S(1)}, bf16[1024,256]{1,0:T(8,128)(2,1)S(1)}, u32[]{:S(2)}, u32[]{:S(2)}) collective-permute-start(bf16[1024,256]{1,0:T(8,128)(2,1)S(1)} %join.1.refs_0_), channel_id=1, source_target_pairs={{0,1},{1,0},{2,3},{3,2},{4,5},{5,4},{6,7},{7,6},{8,9},{9,8},{10,11... | collective-permute-start | bytes 1572872 | tf_op jit(solution)/shard_map/ppermute | solution.py:41
  72.5 14.3 %collective-permute-start.18 = (bf16[1024,256]{1,0:T(8,128)(2,1)S(1)}, bf16[1024,256]{1,0:T(8,128)(2,1)S(1)}, u32[]{:S(2)}, u32[]{:S(2)}) collective-permute-start(bf16[1024,256]{1,0:T(8,128)(2,1)S(1)} %add_0.1.refs_0_.refs_5_), channel_id=1, source_target_pairs={{0,2},{1,3},{2,0},{3,1},{4,6},{5,7},{6,4},{7,5},{8,10},{9,11},{10,... | collective-permute-start | bytes 1572872 | tf_op jit(solution)/shard_map/ppermute | solution.py:47
  85.4 8.1 %collective-permute-start.28 = (bf16[1024,256]{1,0:T(8,128)(2,1)S(1)}, bf16[1024,256]{1,0:T(8,128)(2,1)S(1)}, u32[]{:S(2)}, u32[]{:S(2)}) collective-permute-start(bf16[1024,256]{1,0:T(8,128)(2,1)S(1)} %get-tuple-element.88), channel_id=1, source_target_pairs={{0,1},{1,0},{2,3},{3,2},{4,5},{5,4},{6,7},{7,6},{8,9},{9,8},{10,11... | collective-permute-start | bytes 1572872 | tf_op jit(solution)/shard_map/ppermute | solution.py:41
  86.9 16.0 %collective-permute-start.29 = (bf16[1024,256]{1,0:T(8,128)(2,1)S(1)}, bf16[1024,256]{1,0:T(8,128)(2,1)S(1)}, u32[]{:S(2)}, u32[]{:S(2)}) collective-permute-start(bf16[1024,256]{1,0:T(8,128)(2,1)S(1)} %add_1.1.refs_2_), channel_id=1, source_target_pairs={{0,2},{1,3},{2,0},{3,1},{4,6},{5,7},{6,4},{7,5},{8,10},{9,11},{10,... | collective-permute-start | bytes 1572872 | tf_op jit(solution)/shard_map/ppermute | solution.py:47
  88.9 7.7 %collective-permute-start.21 = (bf16[128,256]{1,0:T(8,128)(2,1)S(1)}, bf16[128,256]{1,0:T(8,128)(2,1)S(1)}, u32[]{:S(2)}, u32[]{:S(2)}) collective-permute-start(bf16[128,256]{1,0:T(8,128)(2,1)S(1)} %get-tuple-element.79), channel_id=1, source_target_pairs={{0,28},{4,24},{8,20},{12,16},{16,12},{20,8},{24,4},{28,0},{1,29},{... | collective-permute-start | bytes 196616 | tf_op jit(solution)/shard_map/ppermute | solution.py:61
  91.1 6.9 %collective-permute-start.22 = (bf16[128,256]{1,0:T(8,128)(2,1)S(1)}, bf16[128,256]{1,0:T(8,128)(2,1)S(1)}, u32[]{:S(2)}, u32[]{:S(2)}) collective-permute-start(bf16[128,256]{1,0:T(8,128)(2,1)S(1)} %get-tuple-element.80), channel_id=1, source_target_pairs={{0,24},{4,28},{8,16},{12,20},{16,8},{20,12},{24,0},{28,4},{1,25},{... | collective-permute-start | bytes 196616 | tf_op jit(solution)/shard_map/ppermute | solution.py:61
  93.4 7.3 %collective-permute-start.23 = (bf16[128,256]{1,0:T(8,128)(2,1)S(1)}, bf16[128,256]{1,0:T(8,128)(2,1)S(1)}, u32[]{:S(2)}, u32[]{:S(2)}) collective-permute-start(bf16[128,256]{1,0:T(8,128)(2,1)S(1)} %get-tuple-element.81), channel_id=1, source_target_pairs={{0,20},{4,16},{8,28},{12,24},{16,4},{20,0},{24,12},{28,8},{1,21},{... | collective-permute-start | bytes 196616 | tf_op jit(solution)/shard_map/ppermute | solution.py:61
  93.5 11.0 %collective-permute-start.24 = (bf16[128,256]{1,0:T(8,128)(2,1)S(1)}, bf16[128,256]{1,0:T(8,128)(2,1)S(1)}, u32[]{:S(2)}, u32[]{:S(2)}) collective-permute-start(bf16[128,256]{1,0:T(8,128)(2,1)S(1)} %get-tuple-element.82), channel_id=1, source_target_pairs={{0,16},{4,20},{8,24},{12,28},{16,0},{20,4},{24,8},{28,12},{1,17},{... | collective-permute-start | bytes 196616 | tf_op jit(solution)/shard_map/ppermute | solution.py:61
  96.7 9.8 %collective-permute-start.25 = (bf16[128,256]{1,0:T(8,128)(2,1)S(1)}, bf16[128,256]{1,0:T(8,128)(2,1)S(1)}, u32[]{:S(2)}, u32[]{:S(2)}) collective-permute-start(bf16[128,256]{1,0:T(8,128)(2,1)S(1)} %get-tuple-element.83), channel_id=1, source_target_pairs={{0,12},{4,8},{8,4},{12,0},{16,28},{20,24},{24,20},{28,16},{1,13},{... | collective-permute-start | bytes 196616 | tf_op jit(solution)/shard_map/ppermute | solution.py:61
  98.0 8.4 %collective-permute-start.26 = (bf16[128,256]{1,0:T(8,128)(2,1)S(1)}, bf16[128,256]{1,0:T(8,128)(2,1)S(1)}, u32[]{:S(2)}, u32[]{:S(2)}) collective-permute-start(bf16[128,256]{1,0:T(8,128)(2,1)S(1)} %get-tuple-element.84), channel_id=1, source_target_pairs={{0,8},{4,12},{8,0},{12,4},{16,24},{20,28},{24,16},{28,20},{1,9},{5... | collective-permute-start | bytes 196616 | tf_op jit(solution)/shard_map/ppermute | solution.py:61
  100.7 10.1 %collective-permute-start.27 = (bf16[128,256]{1,0:T(8,128)(2,1)S(1)}, bf16[128,256]{1,0:T(8,128)(2,1)S(1)}, u32[]{:S(2)}, u32[]{:S(2)}) collective-permute-start(bf16[128,256]{1,0:T(8,128)(2,1)S(1)} %get-tuple-element.85), channel_id=1, source_target_pairs={{0,4},{4,0},{8,12},{12,8},{16,20},{20,16},{24,28},{28,24},{1,5},{5... | collective-permute-start | bytes 196616 | tf_op jit(solution)/shard_map/ppermute | solution.py:61
  103.1 7.8 %collective-permute-start.30 = (bf16[128,256]{1,0:T(8,128)(2,1)S(1)}, bf16[128,256]{1,0:T(8,128)(2,1)S(1)}, u32[]{:S(2)}, u32[]{:S(2)}) collective-permute-start(bf16[128,256]{1,0:T(8,128)(2,1)S(1)} %get-tuple-element.89), channel_id=1, source_target_pairs={{0,28},{4,24},{8,20},{12,16},{16,12},{20,8},{24,4},{28,0},{1,29},{... | collective-permute-start | bytes 196616 | tf_op jit(solution)/shard_map/ppermute | solution.py:61
  104.5 7.8 %collective-permute-start.31 = (bf16[128,256]{1,0:T(8,128)(2,1)S(1)}, bf16[128,256]{1,0:T(8,128)(2,1)S(1)}, u32[]{:S(2)}, u32[]{:S(2)}) collective-permute-start(bf16[128,256]{1,0:T(8,128)(2,1)S(1)} %get-tuple-element.90), channel_id=1, source_target_pairs={{0,24},{4,28},{8,16},{12,20},{16,8},{20,12},{24,0},{28,4},{1,25},{... | collective-permute-start | bytes 196616 | tf_op jit(solution)/shard_map/ppermute | solution.py:61
  106.4 9.8 %collective-permute-start.32 = (bf16[128,256]{1,0:T(8,128)(2,1)S(1)}, bf16[128,256]{1,0:T(8,128)(2,1)S(1)}, u32[]{:S(2)}, u32[]{:S(2)}) collective-permute-start(bf16[128,256]{1,0:T(8,128)(2,1)S(1)} %get-tuple-element.91), channel_id=1, source_target_pairs={{0,20},{4,16},{8,28},{12,24},{16,4},{20,0},{24,12},{28,8},{1,21},{... | collective-permute-start | bytes 196616 | tf_op jit(solution)/shard_map/ppermute | solution.py:61
  106.4 9.8 %collective-permute-start.33 = (bf16[128,256]{1,0:T(8,128)(2,1)S(1)}, bf16[128,256]{1,0:T(8,128)(2,1)S(1)}, u32[]{:S(2)}, u32[]{:S(2)}) collective-permute-start(bf16[128,256]{1,0:T(8,128)(2,1)S(1)} %get-tuple-element.92), channel_id=1, source_target_pairs={{0,16},{4,20},{8,24},{12,28},{16,0},{20,4},{24,8},{28,12},{1,17},{... | collective-permute-start | bytes 196616 | tf_op jit(solution)/shard_map/ppermute | solution.py:61
  110.8 6.9 %collective-permute-start.34 = (bf16[128,256]{1,0:T(8,128)(2,1)S(1)}, bf16[128,256]{1,0:T(8,128)(2,1)S(1)}, u32[]{:S(2)}, u32[]{:S(2)}) collective-permute-start(bf16[128,256]{1,0:T(8,128)(2,1)S(1)} %get-tuple-element.93), channel_id=1, source_target_pairs={{0,12},{4,8},{8,4},{12,0},{16,28},{20,24},{24,20},{28,16},{1,13},{... | collective-permute-start | bytes 196616 | tf_op jit(solution)/shard_map/ppermute | solution.py:61
  110.9 6.9 %collective-permute-start.35 = (bf16[128,256]{1,0:T(8,128)(2,1)S(1)}, bf16[128,256]{1,0:T(8,128)(2,1)S(1)}, u32[]{:S(2)}, u32[]{:S(2)}) collective-permute-start(bf16[128,256]{1,0:T(8,128)(2,1)S(1)} %get-tuple-element.94), channel_id=1, source_target_pairs={{0,8},{4,12},{8,0},{12,4},{16,24},{20,28},{24,16},{28,20},{1,9},{5... | collective-permute-start | bytes 196616 | tf_op jit(solution)/shard_map/ppermute | solution.py:61
  112.3 5.5 %collective-permute-start.36 = (bf16[128,256]{1,0:T(8,128)(2,1)S(1)}, bf16[128,256]{1,0:T(8,128)(2,1)S(1)}, u32[]{:S(2)}, u32[]{:S(2)}) collective-permute-start(bf16[128,256]{1,0:T(8,128)(2,1)S(1)} %get-tuple-element.95), channel_id=1, source_target_pairs={{0,4},{4,0},{8,12},{12,8},{16,20},{20,16},{24,28},{28,24},{1,5},{5... | collective-permute-start | bytes 196616 | tf_op jit(solution)/shard_map/ppermute | solution.py:61
  (15 other events, 117.4 us)

commit v2 on v1

--- a/solution.py
+++ b/solution.py
@@ -238,7 +238,7 @@
             normed_ref[pl.ds(at_row, step), pl.ds(at, width)] = (part * factor).astype(BF16)
         return carry
 
-    lax.fori_loop(0, rows // step, norm, 0)
+    lax.fori_loop(0, rows // step, norm, 0, unroll=True)
     copies[0].wait()
     copies[1].wait()
     tile = min(rows, 1024)

time: 120 us -> 120 us (level)
  transfers between devices with their start and end apart: 38 -> 38, of which waited for: 14 -> 15; matrix products, arithmetic and copies ran while one was open for 0% -> 0% of each run, Pallas kernels for 24% -> 25%
where the time goes in v2:
time: 120 us
  starting transfers between devices  55.7 us (46%)
  Pallas kernels  32.4 us (27%)
  waiting for transfers between devices  26.4 us (22%)
  local copies, waits for them, and re-layouts  5.21 us (4%)
    ppermute x21, starting transfers between devices, exchanged(): moved[s] = lax.ppermute(blocks[s], 'tm', [(i, i ^ s) for i in range(size)])  36.3 us
    pallas_call x2, Pallas kernels, experts(): pl.pallas_call(functools.partial(expert_kernel, local, (0,) * len(parts),...  20.4 us
    ppermute x6, waiting for transfers between devices, from_chip(): return lax.ppermute(x, 'mp', pairs)  11.8 us
    ppermute x6, starting transfers between devices, from_chip(): return lax.ppermute(x, 'mp', pairs)  9.55 us
    ppermute x21, waiting for transfers between devices, exchanged(): moved[s] = lax.ppermute(blocks[s], 'tm', [(i, i ^ s) for i in range(size)])  5.93 us
    ppermute x1, starting transfers between devices, from_behind(): return lax.ppermute(x, axis, pairs)  4.89 us
    ppermute x9, waiting for transfers between devices, core_swap(): return lax.ppermute(x, 'mp', [(i, i ^ 1) for i in range(size)])  4.26 us
    unnamed x20, local copies, waits for them, and re-layouts  4.08 us
  transfers between devices with their start and end apart: 38, of which 15 were waited for; matrix products, arithmetic and copies ran while one was open for 0% of the time, Pallas kernels for 25%

profile of v2, /device:TPU:0, one launch (start us, length us, event | category | flops | bytes accessed | tf_op | source)
XLA Modules:
  0.0 120.1 jit_solution(2822289516928203580)
XLA Ops:
  1.1 4.9 %collective-permute-start = (bf16[2,256,256]{2,1,0:T(8,128)(2,1)S(1)}, bf16[2,256,256]{2,1,0:T(8,128)(2,1)S(1)}, u32[]{:S(2)}, u32[]{:S(2)}) collective-permute-start(bf16[2,256,256]{2,1,0:T(8,128)(2,1)S(1)} %pad_maximum_fusion), channel_id=1, source_target_pairs={{0,4},{4,8},{8,12},{12,16},{16,20},{20,24},{24,28},{1,5},{5,9},{9,... | collective-permute-start | bytes 786440 | tf_op jit(solution)/shard_map/ppermute | solution.py:36
  6.2 3.5 %attend_late.1 = (bf16[256,512]{1,0:T(8,128)(2,1)S(1)}, f32[256,256]{1,0:T(8,128)S(1)}, f32[256,256]{1,0:T(8,128)S(1)}, s32[2,512]{1,0:T(2,128)S(1)}, bf16[512,2...) custom-call(s32[1]{0:T(128)} %bitcast.1.meta_ref, ...), custom_call_target="tpu_custom_call" | custom-call | flops 402653184 | bytes 524288 | tf_op jit(solution)/shard_map/attend_late/pallas_call | solution.py:374
  9.8 1.8 %collective-permute-done.refs_5_ = bf16[2,256,256]{2,1,0:T(8,128)(2,1)S(1)} collective-permute-done((bf16[2,256,256]{2,1,0:T(8,128)(2,1)S(1)}, bf16[2,256,256]{2,1,0:T(8,128)(2,1)S(1)}, u32[]{:S(2)}, u32[]{:S(2)}) %collective-permute-start) | collective-permute-done | bytes 262176 | tf_op jit(solution)/shard_map/ppermute | solution.py:36
  11.6 2.3 %attend_early.1 = (bf16[256,512]{1,0:T(8,128)(2,1)S(1)}, f32[256,256]{1,0:T(8,128)S(1)}, f32[256,256]{1,0:T(8,128)S(1)}) custom-call(s32[1]{0:T(128)} %bitcast.1.meta_ref, s32[4]{0:T(128)S(1)} %pad_add_fusion.order_ref, s32[2,512]{1,0:T(2,128)S(1)} %get-tuple-element.52.refs_0_, bf16[512,256]{1,0:T(8,128)(2,1)S(1)} %get-tuple-element.53.refs_1_, ...), custom_call_target="tpu_custom_call" | custom-call | flops 402653184 | bytes 524288 | tf_op jit(solution)/shard_map/attend_early/pallas_call | solution.py:385
  14.0 1.5 %collective-permute-start.4 = (bf16[256,256]{1,0:T(8,128)(2,1)S(1)}, bf16[256,256]{1,0:T(8,128)(2,1)S(1)}, u32[]{:S(2)}, u32[]{:S(2)}) collective-permute-start(bf16[256,256]{1,0:T(8,128)(2,1)S(1)} %add_late.1), channel_id=1, source_target_pairs={{0,2},{1,3},{2,0},{3,1},{4,6},{5,7},{6,4},{7,5},{8,10},{9,11},{10,... | collective-permute-start | bytes 393224 | tf_op jit(solution)/shard_map/ppermute | solution.py:47
  15.5 1.5 %collective-permute-start.2 = (bf16[256,256]{1,0:T(8,128)(2,1)S(1)}, bf16[256,256]{1,0:T(8,128)(2,1)S(1)}, u32[]{:S(2)}, u32[]{:S(2)}) collective-permute-start(bf16[256,256]{1,0:T(8,128)(2,1)S(1)} %add_early.1), channel_id=1, source_target_pairs={{0,2},{1,3},{2,0},{3,1},{4,6},{5,7},{6,4},{7,5},{8,10},{9,11},{10,... | collective-permute-start | bytes 393224 | tf_op jit(solution)/shard_map/ppermute | solution.py:47
  18.1 2.2 %collective-permute-done.4.refs_5_ = bf16[256,256]{1,0:T(8,128)(2,1)S(1)} collective-permute-done((bf16[256,256]{1,0:T(8,128)(2,1)S(1)}, bf16[256,256]{1,0:T(8,128)(2,1)S(1)}, u32[]{:S(2)}, u32[]{:S(2)}) %collective-permute-start.4) | collective-permute-done | bytes 131104 | tf_op jit(solution)/shard_map/ppermute | solution.py:47
  20.3 2.4 %collective-permute-done.2.refs_2_ = bf16[256,256]{1,0:T(8,128)(2,1)S(1)} collective-permute-done((bf16[256,256]{1,0:T(8,128)(2,1)S(1)}, bf16[256,256]{1,0:T(8,128)(2,1)S(1)}, u32[]{:S(2)}, u32[]{:S(2)}) %collective-permute-start.2) | collective-permute-done | bytes 131104 | tf_op jit(solution)/shard_map/ppermute | solution.py:47
  23.3 1.5 %collective-permute-start.5 = (bf16[512,256]{1,0:T(8,128)(2,1)S(1)}, bf16[512,256]{1,0:T(8,128)(2,1)S(1)}, u32[]{:S(2)}, u32[]{:S(2)}) collective-permute-start(bf16[512,256]{1,0:T(8,128)(2,1)S(1)} %get-tuple-element.64.refs_0_.base_ref), channel_id=1, source_target_pairs={{0,2},{1,3},{2,0},{3,1},{4,6},{5,7},{6,4},{7,5},{8,10},{9,11},{10,... | collective-permute-start | bytes 786440 | tf_op jit(solution)/shard_map/ppermute | solution.py:47
  24.8 4.5 %collective-permute-start.10 = (bf16[128,256]{1,0:T(8,128)(2,1)S(1)}, bf16[128,256]{1,0:T(8,128)(2,1)S(1)}, u32[]{:S(2)}, u32[]{:S(2)}) collective-permute-start(bf16[128,256]{1,0:T(8,128)(2,1)S(1)} %get-tuple-element.70), channel_id=1, source_target_pairs={{0,20},{4,16},{8,28},{12,24},{16,4},{20,0},{24,12},{28,8},{1,21},{... | collective-permute-start | bytes 196616 | tf_op jit(solution)/shard_map/ppermute | solution.py:61
  30.7 3.3 %collective-permute-start.12 = (bf16[128,256]{1,0:T(8,128)(2,1)S(1)}, bf16[128,256]{1,0:T(8,128)(2,1)S(1)}, u32[]{:S(2)}, u32[]{:S(2)}) collective-permute-start(bf16[128,256]{1,0:T(8,128)(2,1)S(1)} %get-tuple-element.72), channel_id=1, source_target_pairs={{0,28},{4,24},{8,20},{12,16},{16,12},{20,8},{24,4},{28,0},{1,29},{... | collective-permute-start | bytes 196616 | tf_op jit(solution)/shard_map/ppermute | solution.py:61
  34.0 2.1 %collective-permute-start.8 = (bf16[128,256]{1,0:T(8,128)(2,1)S(1)}, bf16[128,256]{1,0:T(8,128)(2,1)S(1)}, u32[]{:S(2)}, u32[]{:S(2)}) collective-permute-start(bf16[128,256]{1,0:T(8,128)(2,1)S(1)} %get-tuple-element.68), channel_id=1, source_target_pairs={{0,12},{4,8},{8,4},{12,0},{16,28},{20,24},{24,20},{28,16},{1,13},{... | collective-permute-start | bytes 196616 | tf_op jit(solution)/shard_map/ppermute | solution.py:61
  38.8 1.7 %dispatch.1.refs_8_.refs_7_ = bf16[1024,512]{1,0:T(8,128)(2,1)} custom-call(bf16[512,256]{1,0:T(8,128)(2,1)S(1)} %get-tuple-element.64.refs_0_.base_ref, bf16[512,256]{1,0:T(8,128)(2,1)S(1)} %collective-permute-done.5.refs_0_.refs_1_, f32[128,512]{1,0:T(8,128)S(1)} %get-tuple-element.63.refs_7_.refs_2_), custom_call_target="tpu_custom_call" | custom-call | flops 536870912 | bytes 3145728 | tf_op jit(solution)/shard_map/dispatch/pallas_call | solution.py:429
  40.6 1.4 %collective-permute-done.9.refs_4_ = bf16[128,256]{1,0:T(8,128)(2,1)S(1)} collective-permute-done((bf16[128,256]{1,0:T(8,128)(2,1)S(1)}, bf16[128,256]{1,0:T(8,128)(2,1)S(1)}, u32[]{:S(2)}, u32[]{:S(2)}) %collective-permute-start.9) | collective-permute-done | bytes 65568 | tf_op jit(solution)/shard_map/ppermute | solution.py:61
  43.3 3.8 %all-to-all-start = ((bf16[8,128,512]{2,1,0:T(8,128)(2,1)}), bf16[8,128,512]{2,1,0:T(8,128)(2,1)S(1)}, u32[]{:S(2)}, u32[]{:S(2)}) async-start(bf16[8,128,512]{2,1,0:T(8,128)(2,1)} %bitcast.8), calls=%async_computation | async-start | bytes 2097152 | tf_op jit(solution)/shard_map/all_to_all | solution.py:442
  47.1 6.4 %collective-permute-done.13.refs_1_ = bf16[1024,256]{1,0:T(8,128)(2,1)S(1)} collective-permute-done((bf16[1024,256]{1,0:T(8,128)(2,1)S(1)}, bf16[1024,256]{1,0:T(8,128)(2,1)S(1)}, u32[]{:S(2)}, u32[]{:S(2)}) %collective-permute-start.13) | collective-permute-done | bytes 524320 | tf_op jit(solution)/shard_map/ppermute | solution.py:47
  56.4 10.2 %experts_0.1 = (bf16[1024,256]{1,0:T(8,128)(2,1)S(1)}, bf16[1024,256]{1,0:T(8,128)(2,1)S(1)}, f32[1024,256]{1,0:T(8,128)S(1)}, f32[1024,256]{1,0:T(8,128)S(1)}) custom-call(s32[4]{0:T(128)S(1)} %pad_add_fusion.order_ref, bf16[1024,256]{1,0:T(8,128)(2,1)S(1)} %join.1.refs_0_, bf16[1024,256]{1,0:T(8,128)(2,1)S(1)} %copy-done.4, ...), custom_call_target="tpu_custom_call" | custom-call | flops 6442450944 | bytes 12582912 | tf_op jit(solution)/shard_map/experts_0/pallas_call | solution.py:459
  67.7 1.8 %collective-permute-done.17.got_ref = bf16[1024,256]{1,0:T(8,128)(2,1)S(1)} collective-permute-done((bf16[1024,256]{1,0:T(8,128)(2,1)S(1)}, bf16[1024,256]{1,0:T(8,128)(2,1)S(1)}, u32[]{:S(2)}, u32[]{:S(2)}) %collective-permute-start.17) | collective-permute-done | bytes 524320 | tf_op jit(solution)/shard_map/ppermute | solution.py:41
  69.6 2.7 %all-to-all-done = bf16[8,128,512]{2,1,0:T(8,128)(2,1)S(1)} async-done(((bf16[8,128,512]{2,1,0:T(8,128)(2,1)}), bf16[8,128,512]{2,1,0:T(8,128)(2,1)S(1)}, u32[]{:S(2)}, u32[]{:S(2)}) %all-to-all-start) | async-done | bytes 1048608 | tf_op jit(solution)/shard_map/all_to_all | solution.py:442
  72.5 1.8 %collective-permute-start.18 = (bf16[1024,256]{1,0:T(8,128)(2,1)S(1)}, bf16[1024,256]{1,0:T(8,128)(2,1)S(1)}, u32[]{:S(2)}, u32[]{:S(2)}) collective-permute-start(bf16[1024,256]{1,0:T(8,128)(2,1)S(1)} %add_0.1.refs_0_.refs_5_), channel_id=1, source_target_pairs={{0,2},{1,3},{2,0},{3,1},{4,6},{5,7},{6,4},{7,5},{8,10},{9,11},{10,... | collective-permute-start | bytes 1572872 | tf_op jit(solution)/shard_map/ppermute | solution.py:47
  75.1 10.2 %experts_1.1 = (bf16[1024,256]{1,0:T(8,128)(2,1)S(1)}, bf16[1024,256]{1,0:T(8,128)(2,1)S(1)}, f32[1024,256]{1,0:T(8,128)S(1)}, f32[1024,256]{1,0:T(8,128)S(1)}) custom-call(s32[4]{0:T(128)S(1)} %pad_add_fusion.order_ref, bf16[1024,512]{1,0:T(8,128)(2,1)S(1)} %take.3.refs_0_, bf16[1024,512]{1,0:T(8,128)(2,1)S(1)} %collective-permute-done.19.refs_1_, ...), custom_call_target="tpu_custom_call" | custom-call | flops 6442450944 | bytes 12582912 | tf_op jit(solution)/shard_map/experts_1/pallas_call | solution.py:459
  87.4 2.0 %collective-permute-start.29 = (bf16[1024,256]{1,0:T(8,128)(2,1)S(1)}, bf16[1024,256]{1,0:T(8,128)(2,1)S(1)}, u32[]{:S(2)}, u32[]{:S(2)}) collective-permute-start(bf16[1024,256]{1,0:T(8,128)(2,1)S(1)} %add_1.1.refs_2_), channel_id=1, source_target_pairs={{0,2},{1,3},{2,0},{3,1},{4,6},{5,7},{6,4},{7,5},{8,10},{9,11},{10,... | collective-permute-start | bytes 1572872 | tf_op jit(solution)/shard_map/ppermute | solution.py:47
  89.6 2.2 %collective-permute-start.21 = (bf16[128,256]{1,0:T(8,128)(2,1)S(1)}, bf16[128,256]{1,0:T(8,128)(2,1)S(1)}, u32[]{:S(2)}, u32[]{:S(2)}) collective-permute-start(bf16[128,256]{1,0:T(8,128)(2,1)S(1)} %get-tuple-element.79), channel_id=1, source_target_pairs={{0,28},{4,24},{8,20},{12,16},{16,12},{20,8},{24,4},{28,0},{1,29},{... | collective-permute-start | bytes 196616 | tf_op jit(solution)/shard_map/ppermute | solution.py:61
  91.8 2.4 %collective-permute-start.22 = (bf16[128,256]{1,0:T(8,128)(2,1)S(1)}, bf16[128,256]{1,0:T(8,128)(2,1)S(1)}, u32[]{:S(2)}, u32[]{:S(2)}) collective-permute-start(bf16[128,256]{1,0:T(8,128)(2,1)S(1)} %get-tuple-element.80), channel_id=1, source_target_pairs={{0,24},{4,28},{8,16},{12,20},{16,8},{20,12},{24,0},{28,4},{1,25},{... | collective-permute-start | bytes 196616 | tf_op jit(solution)/shard_map/ppermute | solution.py:61
  94.2 3.2 %collective-permute-start.24 = (bf16[128,256]{1,0:T(8,128)(2,1)S(1)}, bf16[128,256]{1,0:T(8,128)(2,1)S(1)}, u32[]{:S(2)}, u32[]{:S(2)}) collective-permute-start(bf16[128,256]{1,0:T(8,128)(2,1)S(1)} %get-tuple-element.82), channel_id=1, source_target_pairs={{0,16},{4,20},{8,24},{12,28},{16,0},{20,4},{24,8},{28,12},{1,17},{... | collective-permute-start | bytes 196616 | tf_op jit(solution)/shard_map/ppermute | solution.py:61
  100.0 1.5 %collective-permute-done.23.refs_2_ = bf16[128,256]{1,0:T(8,128)(2,1)S(1)} collective-permute-done((bf16[128,256]{1,0:T(8,128)(2,1)S(1)}, bf16[128,256]{1,0:T(8,128)(2,1)S(1)}, u32[]{:S(2)}, u32[]{:S(2)}) %collective-permute-start.23) | collective-permute-done | bytes 65568 | tf_op jit(solution)/shard_map/ppermute | solution.py:61
  101.5 2.2 %collective-permute-start.27 = (bf16[128,256]{1,0:T(8,128)(2,1)S(1)}, bf16[128,256]{1,0:T(8,128)(2,1)S(1)}, u32[]{:S(2)}, u32[]{:S(2)}) collective-permute-start(bf16[128,256]{1,0:T(8,128)(2,1)S(1)} %get-tuple-element.85), channel_id=1, source_target_pairs={{0,4},{4,0},{8,12},{12,8},{16,20},{20,16},{24,28},{28,24},{1,5},{5... | collective-permute-start | bytes 196616 | tf_op jit(solution)/shard_map/ppermute | solution.py:61
  105.3 1.9 %collective-permute-start.31 = (bf16[128,256]{1,0:T(8,128)(2,1)S(1)}, bf16[128,256]{1,0:T(8,128)(2,1)S(1)}, u32[]{:S(2)}, u32[]{:S(2)}) collective-permute-start(bf16[128,256]{1,0:T(8,128)(2,1)S(1)} %get-tuple-element.90), channel_id=1, source_target_pairs={{0,24},{4,28},{8,16},{12,20},{16,8},{20,12},{24,0},{28,4},{1,25},{... | collective-permute-start | bytes 196616 | tf_op jit(solution)/shard_map/ppermute | solution.py:61
  107.2 4.4 %collective-permute-start.33 = (bf16[128,256]{1,0:T(8,128)(2,1)S(1)}, bf16[128,256]{1,0:T(8,128)(2,1)S(1)}, u32[]{:S(2)}, u32[]{:S(2)}) collective-permute-start(bf16[128,256]{1,0:T(8,128)(2,1)S(1)} %get-tuple-element.92), channel_id=1, source_target_pairs={{0,16},{4,20},{8,24},{12,28},{16,0},{20,4},{24,8},{28,12},{1,17},{... | collective-permute-start | bytes 196616 | tf_op jit(solution)/shard_map/ppermute | solution.py:61
  113.0 2.0 %collective-permute-start.36 = (bf16[128,256]{1,0:T(8,128)(2,1)S(1)}, bf16[128,256]{1,0:T(8,128)(2,1)S(1)}, u32[]{:S(2)}, u32[]{:S(2)}) collective-permute-start(bf16[128,256]{1,0:T(8,128)(2,1)S(1)} %get-tuple-element.95), channel_id=1, source_target_pairs={{0,4},{4,0},{8,12},{12,8},{16,20},{20,16},{24,28},{28,24},{1,5},{5... | collective-permute-start | bytes 196616 | tf_op jit(solution)/shard_map/ppermute | solution.py:61
  117.0 1.6 %collective-permute-done.34.refs_4_ = bf16[128,256]{1,0:T(8,128)(2,1)S(1)} collective-permute-done((bf16[128,256]{1,0:T(8,128)(2,1)S(1)}, bf16[128,256]{1,0:T(8,128)(2,1)S(1)}, u32[]{:S(2)}, u32[]{:S(2)}) %collective-permute-start.34) | collective-permute-done | bytes 65568 | tf_op jit(solution)/shard_map/ppermute | solution.py:61
  118.6 1.5 %combine_1.1 = bf16[512,256]{1,0:T(8,128)(2,1)} custom-call(s32[1]{0:T(128)} %bitcast.at_ref, s32[512,2]{1,0:T(8,128)S(1)} %get-tuple-element.51.targets_ref, f32[512,2]{1,0:T(8,128)S(1)} %copy.14.gates_ref, f32[512,256]{1,0:T(8,128)S(1)} %combine_0.1.base_ref, bf16[128,256]{1,0:T(8,128)(2,1)S(1)} %collective-permute-done.30.refs_0_, ...), custom_call_target="tpu_custom_call" | custom-call | flops 536870912 | bytes 3145728 | tf_op jit(solution)/shard_map/combine_1/pallas_call | solution.py:490
  (86 shorter events, 23.5 us)
Async XLA Ops:
  1.1 10.4 %collective-permute-start = (bf16[2,256,256]{2,1,0:T(8,128)(2,1)S(1)}, bf16[2,256,256]{2,1,0:T(8,128)(2,1)S(1)}, u32[]{:S(2)}, u32[]{:S(2)}) collective-permute-start(bf16[2,256,256]{2,1,0:T(8,128)(2,1)S(1)} %pad_maximum_fusion), channel_id=1, source_target_pairs={{0,4},{4,8},{8,12},{12,16},{16,20},{20,24},{24,28},{1,5},{5,9},{9,... | collective-permute-start | bytes 786440 | tf_op jit(solution)/shard_map/ppermute | solution.py:36
  9.7 4.2 %collective-permute-start.3 = (bf16[256,512]{1,0:T(8,128)(2,1)S(1)}, bf16[256,512]{1,0:T(8,128)(2,1)S(1)}, u32[]{:S(2)}, u32[]{:S(2)}) collective-permute-start(bf16[256,512]{1,0:T(8,128)(2,1)S(1)} %get-tuple-element.61), channel_id=1, source_target_pairs={{0,1},{1,0},{2,3},{3,2},{4,5},{5,4},{6,7},{7,6},{8,9},{9,8},{10,11... | collective-permute-start | bytes 786440 | tf_op jit(solution)/shard_map/ppermute | solution.py:41
  14.0 6.4 %collective-permute-start.4 = (bf16[256,256]{1,0:T(8,128)(2,1)S(1)}, bf16[256,256]{1,0:T(8,128)(2,1)S(1)}, u32[]{:S(2)}, u32[]{:S(2)}) collective-permute-start(bf16[256,256]{1,0:T(8,128)(2,1)S(1)} %add_late.1), channel_id=1, source_target_pairs={{0,2},{1,3},{2,0},{3,1},{4,6},{5,7},{6,4},{7,5},{8,10},{9,11},{10,... | collective-permute-start | bytes 393224 | tf_op jit(solution)/shard_map/ppermute | solution.py:47
  15.5 7.2 %collective-permute-start.2 = (bf16[256,256]{1,0:T(8,128)(2,1)S(1)}, bf16[256,256]{1,0:T(8,128)(2,1)S(1)}, u32[]{:S(2)}, u32[]{:S(2)}) collective-permute-start(bf16[256,256]{1,0:T(8,128)(2,1)S(1)} %add_early.1), channel_id=1, source_target_pairs={{0,2},{1,3},{2,0},{3,1},{4,6},{5,7},{6,4},{7,5},{8,10},{9,11},{10,... | collective-permute-start | bytes 393224 | tf_op jit(solution)/shard_map/ppermute | solution.py:47
  23.3 10.7 %collective-permute-start.5 = (bf16[512,256]{1,0:T(8,128)(2,1)S(1)}, bf16[512,256]{1,0:T(8,128)(2,1)S(1)}, u32[]{:S(2)}, u32[]{:S(2)}) collective-permute-start(bf16[512,256]{1,0:T(8,128)(2,1)S(1)} %get-tuple-element.64.refs_0_.base_ref), channel_id=1, source_target_pairs={{0,2},{1,3},{2,0},{3,1},{4,6},{5,7},{6,4},{7,5},{8,10},{9,11},{10,... | collective-permute-start | bytes 786440 | tf_op jit(solution)/shard_map/ppermute | solution.py:47
  24.8 11.3 %collective-permute-start.10 = (bf16[128,256]{1,0:T(8,128)(2,1)S(1)}, bf16[128,256]{1,0:T(8,128)(2,1)S(1)}, u32[]{:S(2)}, u32[]{:S(2)}) collective-permute-start(bf16[128,256]{1,0:T(8,128)(2,1)S(1)} %get-tuple-element.70), channel_id=1, source_target_pairs={{0,20},{4,16},{8,28},{12,24},{16,4},{20,0},{24,12},{28,8},{1,21},{... | collective-permute-start | bytes 196616 | tf_op jit(solution)/shard_map/ppermute | solution.py:61
  29.3 8.1 %collective-permute-start.11 = (bf16[128,256]{1,0:T(8,128)(2,1)S(1)}, bf16[128,256]{1,0:T(8,128)(2,1)S(1)}, u32[]{:S(2)}, u32[]{:S(2)}) collective-permute-start(bf16[128,256]{1,0:T(8,128)(2,1)S(1)} %get-tuple-element.71), channel_id=1, source_target_pairs={{0,24},{4,28},{8,16},{12,20},{16,8},{20,12},{24,0},{28,4},{1,25},{... | collective-permute-start | bytes 196616 | tf_op jit(solution)/shard_map/ppermute | solution.py:61
  30.7 9.9 %collective-permute-start.12 = (bf16[128,256]{1,0:T(8,128)(2,1)S(1)}, bf16[128,256]{1,0:T(8,128)(2,1)S(1)}, u32[]{:S(2)}, u32[]{:S(2)}) collective-permute-start(bf16[128,256]{1,0:T(8,128)(2,1)S(1)} %get-tuple-element.72), channel_id=1, source_target_pairs={{0,28},{4,24},{8,20},{12,16},{16,12},{20,8},{24,4},{28,0},{1,29},{... | collective-permute-start | bytes 196616 | tf_op jit(solution)/shard_map/ppermute | solution.py:61
  34.0 6.6 %collective-permute-start.7 = (bf16[128,256]{1,0:T(8,128)(2,1)S(1)}, bf16[128,256]{1,0:T(8,128)(2,1)S(1)}, u32[]{:S(2)}, u32[]{:S(2)}) collective-permute-start(bf16[128,256]{1,0:T(8,128)(2,1)S(1)} %get-tuple-element.67), channel_id=1, source_target_pairs={{0,8},{4,12},{8,0},{12,4},{16,24},{20,28},{24,16},{28,20},{1,9},{5... | collective-permute-start | bytes 196616 | tf_op jit(solution)/shard_map/ppermute | solution.py:61
  34.0 6.6 %collective-permute-start.8 = (bf16[128,256]{1,0:T(8,128)(2,1)S(1)}, bf16[128,256]{1,0:T(8,128)(2,1)S(1)}, u32[]{:S(2)}, u32[]{:S(2)}) collective-permute-start(bf16[128,256]{1,0:T(8,128)(2,1)S(1)} %get-tuple-element.68), channel_id=1, source_target_pairs={{0,12},{4,8},{8,4},{12,0},{16,28},{20,24},{24,20},{28,16},{1,13},{... | collective-permute-start | bytes 196616 | tf_op jit(solution)/shard_map/ppermute | solution.py:61
  36.1 5.9 %collective-permute-start.9 = (bf16[128,256]{1,0:T(8,128)(2,1)S(1)}, bf16[128,256]{1,0:T(8,128)(2,1)S(1)}, u32[]{:S(2)}, u32[]{:S(2)}) collective-permute-start(bf16[128,256]{1,0:T(8,128)(2,1)S(1)} %get-tuple-element.69), channel_id=1, source_target_pairs={{0,16},{4,20},{8,24},{12,28},{16,0},{20,4},{24,8},{28,12},{1,17},{... | collective-permute-start | bytes 196616 | tf_op jit(solution)/shard_map/ppermute | solution.py:61
  37.4 4.6 %collective-permute-start.6 = (bf16[128,256]{1,0:T(8,128)(2,1)S(1)}, bf16[128,256]{1,0:T(8,128)(2,1)S(1)}, u32[]{:S(2)}, u32[]{:S(2)}) collective-permute-start(bf16[128,256]{1,0:T(8,128)(2,1)S(1)} %take.2), channel_id=1, source_target_pairs={{0,4},{4,0},{8,12},{12,8},{16,20},{20,16},{24,28},{28,24},{1,5},{5... | collective-permute-start | bytes 196616 | tf_op jit(solution)/shard_map/ppermute | solution.py:61
  42.0 11.4 %collective-permute-start.13 = (bf16[1024,256]{1,0:T(8,128)(2,1)S(1)}, bf16[1024,256]{1,0:T(8,128)(2,1)S(1)}, u32[]{:S(2)}, u32[]{:S(2)}) collective-permute-start(bf16[1024,256]{1,0:T(8,128)(2,1)S(1)} %join.1.refs_0_), channel_id=1, source_target_pairs={{0,2},{1,3},{2,0},{3,1},{4,6},{5,7},{6,4},{7,5},{8,10},{9,11},{10,... | collective-permute-start | bytes 1572872 | tf_op jit(solution)/shard_map/ppermute | solution.py:47
  43.3 29.0 %all-to-all-start = ((bf16[8,128,512]{2,1,0:T(8,128)(2,1)}), bf16[8,128,512]{2,1,0:T(8,128)(2,1)S(1)}, u32[]{:S(2)}, u32[]{:S(2)}) async-start(bf16[8,128,512]{2,1,0:T(8,128)(2,1)} %bitcast.8), calls=%async_computation | async-start | bytes 2097152 | tf_op jit(solution)/shard_map/all_to_all | solution.py:442
  47.0 7.2 %collective-permute-start.14 = (bf16[1024,256]{1,0:T(8,128)(2,1)S(1)}, bf16[1024,256]{1,0:T(8,128)(2,1)S(1)}, u32[]{:S(2)}, u32[]{:S(2)}) collective-permute-start(bf16[1024,256]{1,0:T(8,128)(2,1)S(1)} %join.1.refs_0_), channel_id=1, source_target_pairs={{0,1},{1,0},{2,3},{3,2},{4,5},{5,4},{6,7},{7,6},{8,9},{9,8},{10,11... | collective-permute-start | bytes 1572872 | tf_op jit(solution)/shard_map/ppermute | solution.py:41
  72.5 14.3 %collective-permute-start.18 = (bf16[1024,256]{1,0:T(8,128)(2,1)S(1)}, bf16[1024,256]{1,0:T(8,128)(2,1)S(1)}, u32[]{:S(2)}, u32[]{:S(2)}) collective-permute-start(bf16[1024,256]{1,0:T(8,128)(2,1)S(1)} %add_0.1.refs_0_.refs_5_), channel_id=1, source_target_pairs={{0,2},{1,3},{2,0},{3,1},{4,6},{5,7},{6,4},{7,5},{8,10},{9,11},{10,... | collective-permute-start | bytes 1572872 | tf_op jit(solution)/shard_map/ppermute | solution.py:47
  85.9 8.3 %collective-permute-start.28 = (bf16[1024,256]{1,0:T(8,128)(2,1)S(1)}, bf16[1024,256]{1,0:T(8,128)(2,1)S(1)}, u32[]{:S(2)}, u32[]{:S(2)}) collective-permute-start(bf16[1024,256]{1,0:T(8,128)(2,1)S(1)} %get-tuple-element.88), channel_id=1, source_target_pairs={{0,1},{1,0},{2,3},{3,2},{4,5},{5,4},{6,7},{7,6},{8,9},{9,8},{10,11... | collective-permute-start | bytes 1572872 | tf_op jit(solution)/shard_map/ppermute | solution.py:41
  87.4 16.2 %collective-permute-start.29 = (bf16[1024,256]{1,0:T(8,128)(2,1)S(1)}, bf16[1024,256]{1,0:T(8,128)(2,1)S(1)}, u32[]{:S(2)}, u32[]{:S(2)}) collective-permute-start(bf16[1024,256]{1,0:T(8,128)(2,1)S(1)} %add_1.1.refs_2_), channel_id=1, source_target_pairs={{0,2},{1,3},{2,0},{3,1},{4,6},{5,7},{6,4},{7,5},{8,10},{9,11},{10,... | collective-permute-start | bytes 1572872 | tf_op jit(solution)/shard_map/ppermute | solution.py:47
  89.6 7.7 %collective-permute-start.21 = (bf16[128,256]{1,0:T(8,128)(2,1)S(1)}, bf16[128,256]{1,0:T(8,128)(2,1)S(1)}, u32[]{:S(2)}, u32[]{:S(2)}) collective-permute-start(bf16[128,256]{1,0:T(8,128)(2,1)S(1)} %get-tuple-element.79), channel_id=1, source_target_pairs={{0,28},{4,24},{8,20},{12,16},{16,12},{20,8},{24,4},{28,0},{1,29},{... | collective-permute-start | bytes 196616 | tf_op jit(solution)/shard_map/ppermute | solution.py:61
  91.8 6.9 %collective-permute-start.22 = (bf16[128,256]{1,0:T(8,128)(2,1)S(1)}, bf16[128,256]{1,0:T(8,128)(2,1)S(1)}, u32[]{:S(2)}, u32[]{:S(2)}) collective-permute-start(bf16[128,256]{1,0:T(8,128)(2,1)S(1)} %get-tuple-element.80), channel_id=1, source_target_pairs={{0,24},{4,28},{8,16},{12,20},{16,8},{20,12},{24,0},{28,4},{1,25},{... | collective-permute-start | bytes 196616 | tf_op jit(solution)/shard_map/ppermute | solution.py:61
  94.2 7.3 %collective-permute-start.23 = (bf16[128,256]{1,0:T(8,128)(2,1)S(1)}, bf16[128,256]{1,0:T(8,128)(2,1)S(1)}, u32[]{:S(2)}, u32[]{:S(2)}) collective-permute-start(bf16[128,256]{1,0:T(8,128)(2,1)S(1)} %get-tuple-element.81), channel_id=1, source_target_pairs={{0,20},{4,16},{8,28},{12,24},{16,4},{20,0},{24,12},{28,8},{1,21},{... | collective-permute-start | bytes 196616 | tf_op jit(solution)/shard_map/ppermute | solution.py:61
  94.2 11.1 %collective-permute-start.24 = (bf16[128,256]{1,0:T(8,128)(2,1)S(1)}, bf16[128,256]{1,0:T(8,128)(2,1)S(1)}, u32[]{:S(2)}, u32[]{:S(2)}) collective-permute-start(bf16[128,256]{1,0:T(8,128)(2,1)S(1)} %get-tuple-element.82), channel_id=1, source_target_pairs={{0,16},{4,20},{8,24},{12,28},{16,0},{20,4},{24,8},{28,12},{1,17},{... | collective-permute-start | bytes 196616 | tf_op jit(solution)/shard_map/ppermute | solution.py:61
  97.4 9.8 %collective-permute-start.25 = (bf16[128,256]{1,0:T(8,128)(2,1)S(1)}, bf16[128,256]{1,0:T(8,128)(2,1)S(1)}, u32[]{:S(2)}, u32[]{:S(2)}) collective-permute-start(bf16[128,256]{1,0:T(8,128)(2,1)S(1)} %get-tuple-element.83), channel_id=1, source_target_pairs={{0,12},{4,8},{8,4},{12,0},{16,28},{20,24},{24,20},{28,16},{1,13},{... | collective-permute-start | bytes 196616 | tf_op jit(solution)/shard_map/ppermute | solution.py:61
  98.7 8.5 %collective-permute-start.26 = (bf16[128,256]{1,0:T(8,128)(2,1)S(1)}, bf16[128,256]{1,0:T(8,128)(2,1)S(1)}, u32[]{:S(2)}, u32[]{:S(2)}) collective-permute-start(bf16[128,256]{1,0:T(8,128)(2,1)S(1)} %get-tuple-element.84), channel_id=1, source_target_pairs={{0,8},{4,12},{8,0},{12,4},{16,24},{20,28},{24,16},{28,20},{1,9},{5... | collective-permute-start | bytes 196616 | tf_op jit(solution)/shard_map/ppermute | solution.py:61
  101.5 10.1 %collective-permute-start.27 = (bf16[128,256]{1,0:T(8,128)(2,1)S(1)}, bf16[128,256]{1,0:T(8,128)(2,1)S(1)}, u32[]{:S(2)}, u32[]{:S(2)}) collective-permute-start(bf16[128,256]{1,0:T(8,128)(2,1)S(1)} %get-tuple-element.85), channel_id=1, source_target_pairs={{0,4},{4,0},{8,12},{12,8},{16,20},{20,16},{24,28},{28,24},{1,5},{5... | collective-permute-start | bytes 196616 | tf_op jit(solution)/shard_map/ppermute | solution.py:61
  103.8 7.8 %collective-permute-start.30 = (bf16[128,256]{1,0:T(8,128)(2,1)S(1)}, bf16[128,256]{1,0:T(8,128)(2,1)S(1)}, u32[]{:S(2)}, u32[]{:S(2)}) collective-permute-start(bf16[128,256]{1,0:T(8,128)(2,1)S(1)} %get-tuple-element.89), channel_id=1, source_target_pairs={{0,28},{4,24},{8,20},{12,16},{16,12},{20,8},{24,4},{28,0},{1,29},{... | collective-permute-start | bytes 196616 | tf_op jit(solution)/shard_map/ppermute | solution.py:61
  105.3 7.8 %collective-permute-start.31 = (bf16[128,256]{1,0:T(8,128)(2,1)S(1)}, bf16[128,256]{1,0:T(8,128)(2,1)S(1)}, u32[]{:S(2)}, u32[]{:S(2)}) collective-permute-start(bf16[128,256]{1,0:T(8,128)(2,1)S(1)} %get-tuple-element.90), channel_id=1, source_target_pairs={{0,24},{4,28},{8,16},{12,20},{16,8},{20,12},{24,0},{28,4},{1,25},{... | collective-permute-start | bytes 196616 | tf_op jit(solution)/shard_map/ppermute | solution.py:61
  107.2 9.8 %collective-permute-start.32 = (bf16[128,256]{1,0:T(8,128)(2,1)S(1)}, bf16[128,256]{1,0:T(8,128)(2,1)S(1)}, u32[]{:S(2)}, u32[]{:S(2)}) collective-permute-start(bf16[128,256]{1,0:T(8,128)(2,1)S(1)} %get-tuple-element.91), channel_id=1, source_target_pairs={{0,20},{4,16},{8,28},{12,24},{16,4},{20,0},{24,12},{28,8},{1,21},{... | collective-permute-start | bytes 196616 | tf_op jit(solution)/shard_map/ppermute | solution.py:61
  107.2 9.8 %collective-permute-start.33 = (bf16[128,256]{1,0:T(8,128)(2,1)S(1)}, bf16[128,256]{1,0:T(8,128)(2,1)S(1)}, u32[]{:S(2)}, u32[]{:S(2)}) collective-permute-start(bf16[128,256]{1,0:T(8,128)(2,1)S(1)} %get-tuple-element.92), channel_id=1, source_target_pairs={{0,16},{4,20},{8,24},{12,28},{16,0},{20,4},{24,8},{28,12},{1,17},{... | collective-permute-start | bytes 196616 | tf_op jit(solution)/shard_map/ppermute | solution.py:61
  111.6 7.0 %collective-permute-start.34 = (bf16[128,256]{1,0:T(8,128)(2,1)S(1)}, bf16[128,256]{1,0:T(8,128)(2,1)S(1)}, u32[]{:S(2)}, u32[]{:S(2)}) collective-permute-start(bf16[128,256]{1,0:T(8,128)(2,1)S(1)} %get-tuple-element.93), channel_id=1, source_target_pairs={{0,12},{4,8},{8,4},{12,0},{16,28},{20,24},{24,20},{28,16},{1,13},{... | collective-permute-start | bytes 196616 | tf_op jit(solution)/shard_map/ppermute | solution.py:61
  111.6 7.0 %collective-permute-start.35 = (bf16[128,256]{1,0:T(8,128)(2,1)S(1)}, bf16[128,256]{1,0:T(8,128)(2,1)S(1)}, u32[]{:S(2)}, u32[]{:S(2)}) collective-permute-start(bf16[128,256]{1,0:T(8,128)(2,1)S(1)} %get-tuple-element.94), channel_id=1, source_target_pairs={{0,8},{4,12},{8,0},{12,4},{16,24},{20,28},{24,16},{28,20},{1,9},{5... | collective-permute-start | bytes 196616 | tf_op jit(solution)/shard_map/ppermute | solution.py:61
  113.0 5.6 %collective-permute-start.36 = (bf16[128,256]{1,0:T(8,128)(2,1)S(1)}, bf16[128,256]{1,0:T(8,128)(2,1)S(1)}, u32[]{:S(2)}, u32[]{:S(2)}) collective-permute-start(bf16[128,256]{1,0:T(8,128)(2,1)S(1)} %get-tuple-element.95), channel_id=1, source_target_pairs={{0,4},{4,0},{8,12},{12,8},{16,20},{20,16},{24,28},{28,24},{1,5},{5... | collective-permute-start | bytes 196616 | tf_op jit(solution)/shard_map/ppermute | solution.py:61
  (15 other events, 118.4 us)
